TPU v7x, 512 devices: a whole 4x4x16 slice. The times are simulated.
512 devices in a mesh: rep: 64 (over z_hi, y, x), fsdp: 8 (over z_lo, core).
Axes of the slice: x: 4, y: 4, z: 16 (z_hi: 4, z_lo: 4; z = z_hi * 4 + z_lo), core: 2. Of those that a mesh axis runs over, the one named last changes fastest.
Arguments:
- attention_output_features: bfloat16 [131072, 2048], P(('rep', 'fsdp')), may hold values from -6 to 6
- resid: bfloat16 [131072, 4096], P(('rep', 'fsdp')), may hold values from -6 to 6
- adapter_down_weight: float32 [64, 64, 2048], P('rep', None, 'fsdp'), may hold values from -0.125 to 0.125
- adapter_up_weight: float32 [64, 64, 4096], P('rep', None, 'fsdp'), may hold values from -0.75 to 0.75
- adapter_down_moment: float32 [64, 64, 2048], P('rep', None, 'fsdp'), may hold values from -0.15625 to 0.15625
- adapter_down_variance: float32 [64, 64, 2048], P('rep', None, 'fsdp'), may hold values from 1e-06 to 0.0001
- adapter_up_moment: float32 [64, 64, 4096], P('rep', None, 'fsdp'), may hold values from -0.15625 to 0.15625
- adapter_up_variance: float32 [64, 64, 4096], P('rep', None, 'fsdp'), may hold values from 1e-06 to 0.0001
- lengths: int32 [512], P(('rep', 'fsdp')), may hold values from 64 to 256, as said below
- ranks: int32 [64, 8], P('rep'), may hold values from 0 to 7, each once within a row
- gain: bfloat16 [4096], replicated, may hold values from 0.5 to 1.5
- head: float32 [4096], replicated, may hold values from -0.06875 to 0.06875
- step: int32 [1], replicated, may hold values from 0 to 999
Outputs:
- new_lora_a: float32 [64, 64, 2048], P('rep', None, 'fsdp')
- new_lora_b: float32 [64, 64, 4096], P('rep', None, 'fsdp')
- new_moment_a: float32 [64, 64, 2048], P('rep', None, 'fsdp')
- new_second_a: float32 [64, 64, 2048], P('rep', None, 'fsdp')
- new_moment_b: float32 [64, 64, 4096], P('rep', None, 'fsdp')
- new_second_b: float32 [64, 64, 4096], P('rep', None, 'fsdp')
- loss: float32 [64], P('rep')
Inputs may be any that keep to these rules, and one draw needn't show every extreme that they name: `lengths`: each prompt's list holds at least one response of exactly 256 valid tokens.
All inputs are finite; a program needn't handle non-finite values.
Results may differ from a plain program's by a relative error of at most 0.0027.
Values may be sent and summed in bfloat16 or wider, within the bound.
No kernel may reach another device: no remote copies, remote signals or barrier semaphores. Data moves between devices by JAX's collectives and lax.ppermute only.
A program may use at most 64 MiB of HBM per device.

v0:
```python
import jax
import jax.numpy as jnp
from jax import lax
from jax.sharding import PartitionSpec as P


def from_partner(array, axis, distance):
    return lax.ppermute(array, axis, [(i, i ^ 1 << distance) for i in range(lax.axis_size(axis))])


def list_loss(scores, ranking_order):
    ordered = jnp.take_along_axis(scores, ranking_order, axis=1)
    tails = jnp.cumsum(jnp.exp(ordered)[:, ::-1], axis=1)[:, ::-1]
    return jnp.sum(jnp.log(tails) - ordered) / scores.shape[0]


def adamw_optimizer_step(param, moment, second, grad, element_count):
    moment = 0.9 * moment + 0.1 * grad
    second = 0.999 * second + 0.001 * grad * grad
    fix_one = 1.0 - jnp.power(jnp.float32(0.9), element_count)
    fix_two = 1.0 - jnp.power(jnp.float32(0.999), element_count)
    update = moment / fix_one / (jnp.sqrt(second / fix_two) + 1e-08) + 0.01 * param
    return (param - 0.001 * update, moment, second)


def contract_cols(left, piece):
    return lax.dot_general(
        left, piece, (((1,), (1,)), ((), ())), preferred_element_type=jnp.float32
    )


def swap_after(packed, bit):
    return from_partner(packed, "rep", bit)


def bind_bit(sender, bit):

    def apply_swap(packed):
        return sender(packed, bit)

    return apply_swap


def partner_value(sender, packed, step):
    levels = lax.axis_size("rep").bit_length() - 1
    branches = [bind_bit(sender, bit) for bit in range(levels)]
    return lax.switch(step[0] % levels, branches, packed)


def update_both(state, grads, element_count, split_position):
    updated_down_weight, down_first_moment, down_second_moment = adamw_optimizer_step(
        state[0][:, :split_position],
        state[1][:, :split_position],
        state[2][:, :split_position],
        grads[:, :split_position],
        element_count,
    )
    updated_up_weight, up_first_moment, up_second_moment = adamw_optimizer_step(
        state[0][:, split_position:],
        state[1][:, split_position:],
        state[2][:, split_position:],
        grads[:, split_position:],
        element_count,
    )
    return jnp.concatenate(
        [
            jnp.stack([updated_down_weight, down_first_moment, down_second_moment]),
            jnp.stack([updated_up_weight, up_first_moment, up_second_moment]),
        ],
        axis=-1,
    )


def per_device(
    attention_output_features,
    resid,
    adapter_down_weight,
    adapter_up_weight,
    adapter_down_moment,
    adapter_down_variance,
    adapter_up_moment,
    adapter_up_variance,
    lengths,
    ranks,
    gain,
    head,
    step,
):
    split_position = adapter_down_weight.shape[2]
    old_packed = jnp.concatenate(
        [
            jnp.stack([adapter_down_weight[0], adapter_down_moment[0], adapter_down_variance[0]]),
            jnp.stack([adapter_up_weight[0], adapter_up_moment[0], adapter_up_variance[0]]),
        ],
        axis=-1,
    )
    down_half_precision = adapter_down_weight[0].astype(jnp.bfloat16)
    up_half_precision = adapter_up_weight[0].astype(jnp.bfloat16)
    z16 = contract_cols(
        attention_output_features, lax.all_gather(down_half_precision, "fsdp", axis=1, tiled=True)
    ).astype(jnp.bfloat16)
    b_whole = lax.all_gather(up_half_precision, "fsdp", axis=1, tiled=True)
    delta = jnp.dot(z16, b_whole, preferred_element_type=jnp.float32)
    hidden = resid.astype(jnp.float32) + delta
    scale = lax.rsqrt(jnp.mean(hidden * hidden, axis=1, keepdims=True) + 1e-05)
    gainf = gain.astype(jnp.float32)
    tok = jnp.sum(hidden * scale * gainf * head, axis=1).reshape(lengths.shape[0], -1)
    lensf = lengths.astype(jnp.float32)
    valid = (jnp.arange(tok.shape[1], dtype=jnp.int32)[None, :] < lengths[:, None]).astype(
        jnp.float32
    )
    scores_local = jnp.sum(tok * valid, axis=1) / lensf
    scores_all = lax.all_gather(scores_local, "fsdp", axis=0, tiled=True)
    loss, pull = jax.vjp(lambda s: list_loss(s.reshape(ranks.shape), ranks), scores_all)
    dscore_all = pull(jnp.float32(1.0))[0]
    mine = lengths.shape[0]
    dscore = lax.dynamic_slice_in_dim(dscore_all, lax.axis_index("fsdp") * mine, mine)
    dtok = (dscore[:, None] * valid / lensf[:, None]).reshape(-1, 1)
    weighted = dtok * head * gainf
    dh16 = (
        scale * weighted - hidden * scale**3 * jnp.mean(hidden * weighted, axis=1, keepdims=True)
    ).astype(jnp.bfloat16)
    dz = lax.dot_general(
        dh16, b_whole, (((1,), (1,)), ((), ())), preferred_element_type=jnp.float32
    )
    dz16 = dz.astype(jnp.bfloat16)
    term_b = lax.dot_general(
        z16, dh16, (((0,), (0,)), ((), ())), preferred_element_type=jnp.float32
    )
    term_a = lax.dot_general(
        dz16,
        attention_output_features,
        (((0,), (0,)), ((), ())),
        preferred_element_type=jnp.float32,
    )
    down_gradient, up_gradient = (
        lax.psum_scatter(term_a, "fsdp", scatter_dimension=1, tiled=True),
        lax.psum_scatter(term_b, "fsdp", scatter_dimension=1, tiled=True),
    )
    element_count = (step[0] + 1).astype(jnp.float32)
    grads = jnp.concatenate([down_gradient, up_gradient], axis=-1)
    packed = update_both(old_packed, grads, element_count, split_position)
    theirs = partner_value(swap_after, packed, step)
    mixed = (packed + theirs) * 0.5
    left = mixed[:, :, :split_position]
    right = mixed[:, :, split_position:]
    return (
        left[0][None],
        right[0][None],
        left[1][None],
        left[2][None],
        right[1][None],
        right[2][None],
        jnp.reshape(loss, (1,)),
    )


def solution(mesh):
    in_specs = (
        P(("rep", "fsdp"), None),
        P(("rep", "fsdp"), None),
        P("rep", None, "fsdp"),
        P("rep", None, "fsdp"),
        P("rep", None, "fsdp"),
        P("rep", None, "fsdp"),
        P("rep", None, "fsdp"),
        P("rep", None, "fsdp"),
        P(("rep", "fsdp")),
        P("rep", None),
        P(),
        P(),
        P(),
    )
    out_specs = (
        P("rep", None, "fsdp"),
        P("rep", None, "fsdp"),
        P("rep", None, "fsdp"),
        P("rep", None, "fsdp"),
        P("rep", None, "fsdp"),
        P("rep", None, "fsdp"),
        P("rep"),
    )
    return jax.shard_map(
        per_device, mesh=mesh, in_specs=in_specs, out_specs=out_specs, check_vma=False
    )
```

profile of v0, /device:TPU:1, one launch (start us, length us, event | category | flops | bytes accessed | tf_op | source)
XLA Modules:
  0.0 188.7 jit_solution(3092400217464608703)
XLA Ops:
  7.2 0.0 copy-start
  7.2 0.0 reduce-scatter.3.cloned.1.call-start
  7.2 1.0 convert_element_type.39
  8.2 21.7 %all-gather.1 = bf16[1,64,4096]{2,1,0:T(8,128)(2,1)S(1)} all-gather(bf16[1,64,512]{2,1,0:T(8,128)(2,1)S(1)} %convert_element_type.39), channel_id=3, replica_groups=mesh['rep'=64,'fsdp'=8] {'fsdp'}, dimensions={2}, use_global_device_ids=true | all-gather | bytes 589824 | tf_op jit(solution)/shard_map/all_gather | solution.py:102
  30.0 0.9 convert_element_type.36
  30.9 14.4 %all-gather = bf16[1,64,2048]{2,1,0:T(8,128)(2,1)S(1)} all-gather(bf16[1,64,256]{2,1,0:T(8,128)(2,1)S(1)} %convert_element_type.36), channel_id=2, replica_groups=mesh['rep'=64,'fsdp'=8] {'fsdp'}, dimensions={2}, use_global_device_ids=true | all-gather | bytes 294912 | tf_op jit(solution)/shard_map/all_gather | solution.py:100
  45.2 0.0 copy-done
  45.2 0.4 convolution_convert_fusion.1
  45.7 0.0 copy-start.9
  45.7 2.5 %multiply_reduce_fusion.2 = (f32[256]{0:T(256)S(1)}, f32[256,4096]{1,0:T(8,128)S(1)}) fusion(bf16[256,64]{0,1:T(8,128)(2,1)S(1)} %convolution_convert_fusion.1, bf16[1,64,4096]{2,1,0:T(8,128)(2,1)S(1)} %all-gather.1, bf16[256,4096]{1,0:T(8,128)(2,1)} %param.20), kind=kOutput, calls=%fused_computation.7 | convolution fusion | flops 138411776 | bytes 6849536 | tf_op jit(solution)/shard_map/dot_general | solution.py:103
  48.2 0.0 copy-start.1
  48.9 1.2 copy-done.1
  50.1 0.8 multiply_reduce_fusion.1
  50.9 0.6 select_reduce_fusion
  51.5 1.3 dynamic-slice.2
  52.8 1.4 divide_dynamic-update-slice_fusion
  54.2 13.1 %all-reduce = f32[8]{0:T(128)S(1)} all-reduce(f32[8]{0:T(128)S(1)} %divide_dynamic-update-slice_fusion), channel_id=1, replica_groups=mesh['rep'=64,'fsdp'=8] {'fsdp'}, use_global_device_ids=true, to_apply=%add | all-reduce | flops 8 | bytes 64
  67.3 0.6 gather_fusion
  67.9 0.1 rev.12
  68.0 0.2 reduce_window_sum.22
  68.2 0.1 rev.15
  68.3 0.2 reduce_window_sum.23
  68.5 0.1 rev.14
  68.6 0.6 subtract_reduce_fusion
  69.2 0.6 scatter_custom_fusion
  69.9 0.6 dynamic-slice.1
  70.4 0.9 select_divide_fusion
  71.4 2.9 %multiply_reduce_fusion = f32[256]{0:T(256)S(1)} fusion(f32[256,4096]{1,0:T(8,128)} %copy-done.1, f32[256]{0:T(256)S(1)} %select_divide_fusion, f32[4096]{0:T(1024)S(1)} %copy-done.6, f32[4096]{0:T(1024)S(1)} %convert_element_type.41), kind=kLoop, calls=%fused_computation.4 | loop fusion | flops 4194048 | bytes 4229120 | tf_op jit(solution)/shard_map/reduce_sum | solution.py:121
  74.3 1.5 subtract_convert_fusion
  75.8 0.0 copy-start.4
  75.8 0.0 copy-start.5
  75.8 0.0 copy-start.7
  75.8 3.2 %fusion = f32[64,2048]{1,0:T(8,128)} fusion(bf16[256,2048]{1,0:T(8,128)(2,1)S(1)} %copy-done, bf16[256,4096]{1,0:T(8,128)(2,1)S(1)} %subtract_convert_fusion, bf16[1,64,4096]{2,1,0:T(8,128)(2,1)} %copy-done.3), kind=kOutput, calls=%fused_computation.9 | convolution fusion | flops 201342976 | bytes 4194304 | tf_op jit(solution)/shard_map/dot_general | solution.py:130
  79.0 0.0 reduce-scatter.3.cloned.1.call-update
  79.0 0.0 reduce-scatter.5.cloned.1.call-start
  79.1 1.5 fusion.19
  80.6 0.0 reduce-scatter.5.cloned.1.call-update
  81.4 1.0 maximum_maximum_fusion
  82.4 36.5 %reduce-scatter.3.cloned.1.call-done = f32[64,256]{1,0:T(8,128)} async-done(((f32[64,2048]{1,0:T(8,128)}), f32[64,256]{1,0:T(8,128)}) %reduce-scatter.3.cloned.1.call-update) | async-done | bytes 65552 | tf_op jit(solution)/shard_map/reduce_scatter | solution.py:137
  118.9 0.9 subtract_bitcast_fusion.1
  119.9 43.2 %reduce-scatter.5.cloned.1.call-done = f32[64,512]{1,0:T(8,128)} async-done(((f32[64,4096]{1,0:T(8,128)}), f32[64,512]{1,0:T(8,128)}) %reduce-scatter.5.cloned.1.call-update) | async-done | bytes 131088 | tf_op jit(solution)/shard_map/reduce_scatter | solution.py:138
  163.1 1.0 subtract_bitcast_fusion
  164.1 15.1 %conditional.1 = (f32[3,64,768]{2,1,0:T(8,128)}) conditional(s32[]{:T(128)} %clamp.3, f32[3,64,768]{2,1,0:T(8,128)S(1)} %maximum_maximum_fusion.1, f32[3,64,768]{2,1,0:T(8,128)S(1)} %maximum_maximum_fusion.1, f32[3,64,768]{2,1,0:T(8,128)S(1)} %maximum_maximum_fusion.1, ...), branch_computations={%region_9.10_spmd, %region_10.11_spmd, %region_11.12_spmd, %region... | conditional | bytes 2359344 | solution.py:47
  164.2 3.9 %collective-permute-start.3 = (f32[3,64,768]{2,1,0:T(8,128)S(1)}, f32[3,64,768]{2,1,0:T(8,128)}, u32[]{:S(2)}, u32[]{:S(2)}) collective-permute-start(f32[3,64,768]{2,1,0:T(8,128)S(1)} %param.3), channel_id=1, source_target_pairs={{0,64},{8,72},{16,80},{24,88},{32,96},{40,104},{48,112},{56,120},{... | collective-permute-start | bytes 1769480 | tf_op jit(solution)/shard_map/cond/branch_3_fun/ppermute | solution.py:8
  168.1 11.2 %collective-permute-done.3 = f32[3,64,768]{2,1,0:T(8,128)} collective-permute-done((f32[3,64,768]{2,1,0:T(8,128)S(1)}, f32[3,64,768]{2,1,0:T(8,128)}, u32[]{:S(2)}, u32[]{:S(2)}) %collective-permute-start.3) | collective-permute-done | bytes 589856 | tf_op jit(solution)/shard_map/cond/branch_3_fun/ppermute | solution.py:8
  179.3 1.1 add_multiply_fusion
  180.4 0.8 fusion.17
  181.1 0.7 fusion.18
  (22 shorter events, 0.2 us)
Async XLA Ops:
  7.2 38.1 %copy-start = (bf16[256,2048]{1,0:T(8,128)(2,1)S(1)}, bf16[256,2048]{1,0:T(8,128)(2,1)}, u32[]{:S(2)}) copy-start(bf16[256,2048]{1,0:T(8,128)(2,1)} %param.19) | copy-start | bytes 3145732
  7.2 111.8 %reduce-scatter.3.cloned.1.call-start = ((), (), s32[]{:S(2)}) async-start(), calls=%async_computation.2 | async-start | bytes 589824 | tf_op jit(solution)/shard_map/reduce_scatter | solution.py:137
  30.0 18.2 %copy-start.3 = (bf16[1,64,4096]{2,1,0:T(8,128)(2,1)}, bf16[1,64,4096]{2,1,0:T(8,128)(2,1)S(1)}, u32[]{:S(2)}) copy-start(bf16[1,64,4096]{2,1,0:T(8,128)(2,1)S(1)} %all-gather.1) | copy-start | bytes 1572868
  30.9 17.3 %copy-start.8 = (bf16[4096]{0:T(1024)(128)(2,1)S(1)}, bf16[4096]{0:T(1024)(128)(2,1)}, u32[]{:S(2)}) copy-start(bf16[4096]{0:T(1024)(128)(2,1)} %param.29) | copy-start | bytes 24580
  30.9 19.2 %copy-start.6 = (f32[4096]{0:T(1024)S(1)}, f32[4096]{0:T(1024)}, u32[]{:S(2)}) copy-start(f32[4096]{0:T(1024)} %param.30) | copy-start | bytes 49156
  45.7 21.6 %copy-start.9 = (s32[1,8]{1,0:T(1,128)S(1)}, s32[1,8]{1,0:T(1,128)}, u32[]{:S(2)}) copy-start(s32[1,8]{1,0:T(1,128)} %param.28) | copy-start | bytes 100
  48.2 1.9 %copy-start.1 = (f32[256,4096]{1,0:T(8,128)}, f32[256,4096]{1,0:T(8,128)S(1)}, u32[]{:S(2)}) copy-start(f32[256,4096]{1,0:T(8,128)S(1)} %get-tuple-element.42) | copy-start | bytes 12582916
  69.8 4.5 %copy-start.2 = (f32[256,4096]{1,0:T(8,128)S(1)}, f32[256,4096]{1,0:T(8,128)}, u32[]{:S(2)}) copy-start(f32[256,4096]{1,0:T(8,128)} %copy-done.1) | copy-start | bytes 12582916
  75.8 5.5 %copy-start.4 = (f32[1,64,512]{2,1,0:T(8,128)S(1)}, f32[1,64,512]{2,1,0:T(8,128)}, u32[]{:S(2)}) copy-start(f32[1,64,512]{2,1,0:T(8,128)} %param.22) | copy-start | bytes 393220
  75.8 5.5 %copy-start.5 = (f32[1,64,256]{2,1,0:T(8,128)S(1)}, f32[1,64,256]{2,1,0:T(8,128)}, u32[]{:S(2)}) copy-start(f32[1,64,256]{2,1,0:T(8,128)} %param.21) | copy-start | bytes 196612
  75.8 5.5 %copy-start.7 = (f32[1,64,512]{2,1,0:T(8,128)S(1)}, f32[1,64,512]{2,1,0:T(8,128)}, u32[]{:S(2)}) copy-start(f32[1,64,512]{2,1,0:T(8,128)} %param.26) | copy-start | bytes 393220
  79.0 84.0 %reduce-scatter.5.cloned.1.call-start = ((), (), s32[]{:S(2)}) async-start(), calls=%async_computation.3 | async-start | bytes 1179648 | tf_op jit(solution)/shard_map/reduce_scatter | solution.py:138
  164.2 15.1 %collective-permute-start.3 = (f32[3,64,768]{2,1,0:T(8,128)S(1)}, f32[3,64,768]{2,1,0:T(8,128)}, u32[]{:S(2)}, u32[]{:S(2)}) collective-permute-start(f32[3,64,768]{2,1,0:T(8,128)S(1)} %param.3), channel_id=1, source_target_pairs={{0,64},{8,72},{16,80},{24,88},{32,96},{40,104},{48,112},{56,120},{... | collective-permute-start | bytes 1769480 | tf_op jit(solution)/shard_map/cond/branch_3_fun/ppermute | solution.py:8
Sparse Core Ops, SparseCore 0:
  79.2 39.7 reduce-scatter.2
  122.0 41.0 reduce-scatter.4
where the time goes:
time: 191 us; the launch traced here: 189 us
  waiting for transfers between devices  91 us (48%)
  blocking collectives  49.2 us (26%)
  other arithmetic  15.8 us (8%)
  between operations  15.7 us (8%)
  matrix products  7.54 us (4%)
  local copies, waits for them, and re-layouts  5.51 us (3%)
  starting transfers between devices  4.01 us (2%)
    reduce_scatter x1, waiting for transfers between devices, per_device(): lax.psum_scatter(term_b, 'fsdp', scatter_dimension=1, tiled=True)  43.2 us
    reduce_scatter x1, waiting for transfers between devices, per_device(): lax.psum_scatter(term_a, 'fsdp', scatter_dimension=1, tiled=True)  36.5 us
    all_gather x1, blocking collectives, per_device(): b_whole = lax.all_gather(up_half_precision, 'fsdp', axis=1, tiled=True)  21.7 us
    all_gather x1, blocking collectives, per_device(): lax.all_gather(down_half_precision, 'fsdp', axis=1, tiled=True)  14.4 us
    unnamed x1, blocking collectives  13.1 us
    ppermute x1, waiting for transfers between devices, from_partner(): lax.ppermute(array, axis, [(i, i ^ 1 << distance) for i in range(lax.axis...  11.2 us
    ppermute x1, starting transfers between devices, from_partner(): lax.ppermute(array, axis, [(i, i ^ 1 << distance) for i in range(lax.axis...  3.93 us
  transfers between devices with their start and end apart: 3, of which 3 were waited for; matrix products, arithmetic and copies ran while one was open for 2% of the time, Pallas kernels for 0%

commit v1 on v0

v1 whole, which is shorter than its diff:
```python
import jax
import jax.numpy as jnp
import numpy as np
from jax import lax
from jax.experimental import pallas as pl
from jax.experimental.pallas import tpu as pltpu
from jax.sharding import PartitionSpec as P

F32 = jnp.float32
BF16 = jnp.bfloat16
RANK = 64
LANES = 128
TAIL = 16
COUNT_BITS = 10
VMEM = pl.BlockSpec(memory_space=pltpu.VMEM)
SMEM = pl.BlockSpec(memory_space=pltpu.SMEM)


def nt(left, right):
    return lax.dot_general(left, right, (((1,), (1,)), ((), ())), preferred_element_type=F32)


def tn(left, right):
    return lax.dot_general(left, right, (((0,), (0,)), ((), ())), preferred_element_type=F32)


def nn(left, right):
    return lax.dot_general(left, right, (((1,), (0,)), ((), ())), preferred_element_type=F32)


def split_two(value):
    high = value.astype(BF16)
    return high, (value - high.astype(F32)).astype(BF16)


def split_three(value):
    high = value.astype(BF16)
    rest = value - high.astype(F32)
    middle = rest.astype(BF16)
    return high, middle, (rest - middle.astype(F32)).astype(BF16)


def fold_rows(stacked):
    half = stacked.shape[0] // 2
    return stacked[:half] + stacked[half:]


def gradient_terms(length_ref, x_ref, r_ref, weights_ref, gain_ref, head_ref, out_ref):
    shards = out_ref.shape[0]
    tokens, width = r_ref.shape
    down_cols = x_ref.shape[1] // shards
    up_cols = width // shards
    w = gain_ref[...].astype(F32) * head_ref[...]
    w_high, w_middle, w_low = split_three(w)
    row = lax.broadcasted_iota(jnp.int32, (TAIL, width), 0)
    w_rows = jnp.where(
        row == 0,
        w_high.astype(F32),
        jnp.where(row == 1, w_middle.astype(F32), jnp.where(row == 2, w_low.astype(F32), 0.0)),
    ).astype(BF16)

    def down(shard):
        return weights_ref[shard % 2, shard // 2, :, :down_cols]

    def up(shard):
        return weights_ref[shard % 2, shard // 2, :, down_cols:]

    z = jnp.zeros((tokens, RANK), F32)
    p_ext = jnp.zeros((tokens, RANK + TAIL), F32)
    gram = jnp.zeros((RANK + TAIL, RANK + TAIL), F32)
    for f in range(shards):
        z += nt(x_ref[:, f * down_cols : (f + 1) * down_cols], down(f))
        cols = slice(f * up_cols, (f + 1) * up_cols)
        b_ext = jnp.concatenate([up(f), w_rows[:, cols]], axis=0)
        p_ext += nt(r_ref[:, cols], b_ext)
        gram += nt(b_ext, b_ext)
    squares = jnp.zeros((tokens, LANES), F32)
    for c in range(width // LANES):
        piece = r_ref[:, c * LANES : (c + 1) * LANES].astype(F32)
        squares += piece * piece
    squares = jnp.sum(squares, axis=1, keepdims=True)

    z16 = z.astype(BF16)
    zf = z16.astype(F32)
    p = p_ext[:, :RANK]
    m_high, m_middle, m_low = split_three(gram[:RANK, :RANK])
    v = p + (nn(z16, m_high) + (nn(z16, m_middle) + nn(z16, m_low)))
    bw = jnp.sum(gram[RANK : RANK + 3, :RANK], axis=0, keepdims=True)
    rw = jnp.sum(p_ext[:, RANK : RANK + 3], axis=1, keepdims=True)
    total = squares + jnp.sum(zf * (p + v), axis=1, keepdims=True)
    along = rw + jnp.sum(zf * bw, axis=1, keepdims=True)
    scale = lax.rsqrt(total * (1.0 / width) + 1e-05)

    length = length_ref[0]
    token = lax.broadcasted_iota(jnp.int32, (tokens, 1), 0)
    over = jnp.where(token < length, 1.0 / jnp.full((tokens, 1), length, jnp.int32).astype(F32), 0.0)
    score = jnp.sum(over * scale * along, axis=0, keepdims=True)
    alpha = over * scale
    beta = over * scale * scale * scale * along * (1.0 / width)

    dz = jnp.concatenate(split_two(alpha * bw - beta * v), axis=1)
    bz = jnp.concatenate(split_two(beta * zf), axis=1)
    az = jnp.concatenate(split_two(alpha * zf), axis=1)
    az_sum = fold_rows(tn(az, jnp.ones((tokens, LANES), BF16)))
    inner = jnp.concatenate(split_two(fold_rows(tn(bz, z16))), axis=0)
    s_high, s_middle, s_low = split_three(jnp.broadcast_to(score, (TAIL, LANES)))
    tail_row = lax.broadcasted_iota(jnp.int32, (TAIL, LANES), 0)
    tail = jnp.where(
        tail_row == 0,
        s_high.astype(F32),
        jnp.where(tail_row == 1, s_middle.astype(F32), s_low.astype(F32)),
    ).astype(BF16)
    for f in range(shards):
        term_a = fold_rows(tn(dz, x_ref[:, f * down_cols : (f + 1) * down_cols])).astype(BF16)
        at = 0
        for c in range(down_cols // LANES):
            out_ref[f, at : at + RANK, :] = term_a[:, c * LANES : (c + 1) * LANES]
            at += RANK
        term_b = fold_rows(
            tn(bz, r_ref[:, f * up_cols : (f + 1) * up_cols]) + nn(inner, up(f))
        )
        for c in range(up_cols // LANES):
            first = f * up_cols + c * LANES
            out_ref[f, at : at + RANK, :] = (
                az_sum * w[:, first : first + LANES] - term_b[:, c * LANES : (c + 1) * LANES]
            ).astype(BF16)
            at += RANK
        out_ref[f, at : at + TAIL, :] = tail


def power_gap(base, count):
    factor = float(np.float32(base))
    gap = jnp.float32(0.0)
    for bit in range(COUNT_BITS):
        part = jnp.float32(1.0 - factor ** (2**bit))
        gap = jnp.where((count >> bit) & 1 == 1, gap + part - gap * part, gap)
    return gap


def update(
    ranks_ref, step_ref, terms_ref, a_ref, ma_ref, va_ref, b_ref, mb_ref, vb_ref,
    na_ref, nma_ref, nva_ref, nb_ref, nmb_ref, nvb_ref, packed_ref, loss_ref,
):
    shards = terms_ref.shape[0]
    base = terms_ref.shape[1] - TAIL
    square = (shards, LANES)
    sublane = lax.broadcasted_iota(jnp.int32, square, 0)
    lane = lax.broadcasted_iota(jnp.int32, square, 1)
    score_col = jnp.zeros(square, F32)
    score_row = jnp.zeros(square, F32)
    place_col = jnp.zeros(square, jnp.int32)
    place_row = jnp.zeros(square, jnp.int32)
    for d in range(shards):
        parts = terms_ref[d, base : base + TAIL, :].astype(F32)
        one = jnp.broadcast_to(parts[0:1] + (parts[1:2] + parts[2:3]), square)
        score_col = jnp.where(sublane == d, one, score_col)
        score_row = jnp.where(lane == d, one, score_row)
        place_col = jnp.where(sublane == ranks_ref[0, d], d, place_col)
        place_row = jnp.where(lane == ranks_ref[0, d], d, place_row)
    live = lane < shards
    after = jnp.where(live & (place_col >= place_row), 1.0, 0.0)
    weight = jnp.exp(score_col)
    tails = jnp.where(live[:1], jnp.sum(after * weight, axis=0, keepdims=True), 1.0)
    losses = jnp.where(live[:1], jnp.log(tails) - score_row[:1], 0.0)
    loss_ref[0] = jnp.sum(losses)
    pull = jnp.sum(after * (weight / tails), axis=1, keepdims=True) - 1.0

    count = step_ref[0] + 1
    one_fix = 1.0 / jnp.full((RANK, LANES), power_gap(0.9, count), F32)
    two_fix = 1.0 / jnp.full((RANK, LANES), power_gap(0.999, count), F32)
    at = 0
    for refs in (
        (a_ref, ma_ref, va_ref, na_ref, nma_ref, nva_ref),
        (b_ref, mb_ref, vb_ref, nb_ref, nmb_ref, nvb_ref),
    ):
        for c in range(refs[0].shape[2] // LANES):
            cols = slice(c * LANES, (c + 1) * LANES)
            grad = jnp.zeros((RANK, LANES), F32)
            for d in range(shards):
                grad += pull[d : d + 1] * terms_ref[d, at : at + RANK, :].astype(F32)
            param = refs[0][0, :, cols]
            moment = 0.9 * refs[1][0, :, cols] + 0.1 * grad
            second = 0.999 * refs[2][0, :, cols] + 0.001 * grad * grad
            change = moment * one_fix / (jnp.sqrt(second * two_fix) + 1e-08) + 0.01 * param
            param = param - 0.001 * change
            for i, value in enumerate((param, moment, second)):
                refs[3 + i][0, :, cols] = value
                packed_ref[i, at : at + RANK, :] = value.astype(BF16)
            at += RANK


def average(theirs_ref, *refs):
    mine, out = refs[:6], refs[6:]
    for i in range(3):
        at = 0
        for array in (i, 3 + i):
            for c in range(mine[array].shape[2] // LANES):
                cols = slice(c * LANES, (c + 1) * LANES)
                out[array][0, :, cols] = 0.5 * (
                    mine[array][0, :, cols] + theirs_ref[i, at : at + RANK, :].astype(F32)
                )
                at += RANK


def partner_swap(bit):

    def swap(packed):
        size = lax.axis_size("rep")
        return lax.ppermute(packed, "rep", [(i, i ^ 1 << bit) for i in range(size)])

    return swap


def gather_weights(packed):
    size = lax.axis_size("fsdp")
    same_core = [list(range(core, size, 2)) for core in range(2)]
    same_chip = [[first, first + 1] for first in range(0, size, 2)]
    across = lax.all_gather(packed, "fsdp", axis_index_groups=same_core)
    return lax.all_gather(across, "fsdp", axis_index_groups=same_chip)


def per_device(
    features, resid, down_weight, up_weight, down_moment, down_variance, up_moment, up_variance,
    lengths, ranks, gain, head, step,
):
    shards = lax.axis_size("fsdp")
    levels = lax.axis_size("rep").bit_length() - 1
    width = resid.shape[1]
    panels = (down_weight.shape[2] + up_weight.shape[2]) // LANES
    packed = jnp.concatenate([down_weight[0], up_weight[0]], axis=1).astype(BF16)
    weights = gather_weights(packed)
    terms = pl.pallas_call(
        gradient_terms,
        out_shape=jax.ShapeDtypeStruct((shards, panels * RANK + TAIL, LANES), BF16),
        in_specs=[SMEM] + [VMEM] * 5,
        out_specs=VMEM,
        compiler_params=pltpu.CompilerParams(vmem_limit_bytes=32 * 2**20),
        name="gradient_terms",
    )(lengths, features, resid, weights, gain.reshape(1, width), head.reshape(1, width))
    terms = lax.all_to_all(terms, "fsdp", 0, 0)
    state = (down_weight, down_moment, down_variance, up_weight, up_moment, up_variance)
    outs = pl.pallas_call(
        update,
        out_shape=[jax.ShapeDtypeStruct(s.shape, F32) for s in state]
        + [
            jax.ShapeDtypeStruct((3, panels * RANK, LANES), BF16),
            jax.ShapeDtypeStruct((1,), F32),
        ],
        in_specs=[SMEM, SMEM] + [VMEM] * 7,
        out_specs=[VMEM] * 7 + [SMEM],
        compiler_params=pltpu.CompilerParams(vmem_limit_bytes=32 * 2**20),
        name="update",
    )(ranks, step, terms, *state)
    mine, mine_packed, loss = outs[:6], outs[6], outs[7]
    theirs = lax.switch(step[0] % levels, [partner_swap(bit) for bit in range(levels)], mine_packed)
    mixed = pl.pallas_call(
        average,
        out_shape=[jax.ShapeDtypeStruct(s.shape, F32) for s in state],
        in_specs=[VMEM] * 7,
        out_specs=[VMEM] * 6,
        compiler_params=pltpu.CompilerParams(vmem_limit_bytes=32 * 2**20),
        name="average",
    )(theirs, *mine)
    new_a, new_ma, new_va, new_b, new_mb, new_vb = mixed
    return new_a, new_b, new_ma, new_va, new_mb, new_vb, loss


def solution(mesh):
    rows = P(("rep", "fsdp"), None)
    cols = P("rep", None, "fsdp")
    in_specs = (rows, rows) + (cols,) * 6 + (P(("rep", "fsdp")), P("rep", None), P(), P(), P())
    out_specs = (cols,) * 6 + (P("rep"),)
    return jax.shard_map(
        per_device, mesh=mesh, in_specs=in_specs, out_specs=out_specs, check_vma=False
    )
```

time: 191 us -> 95.7 us (0.50); the launches traced: 189 us -> 95.3 us
  waiting for transfers between devices: 91 us -> 45.5 us
  blocking collectives: 49.2 us -> 24 us
  other arithmetic: 15.8 us -> 1.77 us
  between operations: 15.7 us -> 2.21 us
  starting transfers between devices: 4.01 us -> 13.1 us
  matrix products: 7.54 us -> 0 us
  Pallas kernels: 0 us -> 6.84 us
  local copies, waits for them, and re-layouts: 5.51 us -> 1.98 us
    reduce_scatter x2 -> x0, waiting for transfers between devices: 79.8 us -> none  [the longest x1 43.2 us: per_device(): lax.psum_scatter(term_b, 'fsdp', scatter_dimension=1, tiled=True)]
    all_to_all x0 -> x1, waiting for transfers between devices: none -> 20.2 us  [per_device(): terms = lax.all_to_all(terms, 'fsdp', 0, 0)]
    ppermute x1, waiting for transfers between devices: 11.2 us -> 25.3 us  [swap(): return lax.ppermute(packed, 'rep', [(i, i ^ 1 << bit) for i in range(size)])]
    unnamed x1 -> x0, blocking collectives: 13.1 us -> none
    all_gather x2, blocking collectives: 36.1 us -> 24 us  [the longest x1 14.4 us: gather_weights(): across = lax.all_gather(packed, 'fsdp', axis_index_groups=same_core)]
    dot_general x4 -> x0, matrix products: 7.54 us -> none  [the longest x1 3.17 us: per_device(): lax.dot_general(dz16, attention_output_features, (((0,), (0,)), ((), ()))...]
    pallas_call x0 -> x3, Pallas kernels: none -> 6.84 us  [the longest x1 3.83 us: per_device(): pl.pallas_call(gradient_terms, out_shape=jax.ShapeDtypeStruct((shards, pa...]
    ppermute x1, starting transfers between devices: 3.93 us -> 9.24 us  [swap(): return lax.ppermute(packed, 'rep', [(i, i ^ 1 << bit) for i in range(size)])]
  transfers between devices with their start and end apart: 3 -> 2, of which waited for: 3 -> 2; matrix products, arithmetic and copies ran while one was open for 2% -> 0% of each run, Pallas kernels for 0% -> 0%
where the time goes in v1:
time: 95.7 us; the launch traced here: 95.3 us
  waiting for transfers between devices  45.5 us (48%)
  blocking collectives  24 us (25%)
  starting transfers between devices  13.1 us (14%)
  Pallas kernels  6.84 us (7%)
  between operations  2.21 us (2%)
  local copies, waits for them, and re-layouts  1.98 us (2%)
  other arithmetic  1.77 us (2%)
    ppermute x1, waiting for transfers between devices, swap(): return lax.ppermute(packed, 'rep', [(i, i ^ 1 << bit) for i in range(size)])  25.3 us
    all_to_all x1, waiting for transfers between devices, per_device(): terms = lax.all_to_all(terms, 'fsdp', 0, 0)  20.2 us
    all_gather x1, blocking collectives, gather_weights(): across = lax.all_gather(packed, 'fsdp', axis_index_groups=same_core)  14.4 us
    all_gather x1, blocking collectives, gather_weights(): return lax.all_gather(across, 'fsdp', axis_index_groups=same_chip)  9.6 us
    ppermute x1, starting transfers between devices, swap(): return lax.ppermute(packed, 'rep', [(i, i ^ 1 << bit) for i in range(size)])  9.24 us
    pallas_call x1, Pallas kernels, per_device(): pl.pallas_call(gradient_terms, out_shape=jax.ShapeDtypeStruct((shards, pa...  3.83 us
    all_to_all x1, starting transfers between devices, per_device(): terms = lax.all_to_all(terms, 'fsdp', 0, 0)  3.82 us
  transfers between devices with their start and end apart: 2, of which 2 were waited for; matrix products, arithmetic and copies ran while one was open for 0% of the time, Pallas kernels for 0%

profile of v1, /device:TPU:1, one launch (start us, length us, event | category | flops | bytes accessed | tf_op | source)
XLA Modules:
  0.0 95.3 jit_solution(8413099601806396429)
XLA Ops:
  0.6 0.0 copy-start.8
  0.6 0.0 copy-start
  1.4 0.7 reshape.47.gain_ref
  2.2 0.8 convert.6
  3.0 0.9 convert.7
  3.9 14.4 %all_gather.10 = bf16[4,64,768]{2,1,0:T(8,128)(2,1)S(1)} all-gather(bf16[1,64,768]{2,1,0:T(8,128)(2,1)S(1)} %pad_maximum_fusion), channel_id=1, replica_groups={{0,2,4,6},{1,3,5,7},{8,10,12,14},{9,11,13,15},{16,18,20,22},{17,19,21,2..., dimensions={0}, use_global_device_ids=true | all-gather | bytes 491520 | tf_op jit(solution)/shard_map/all_gather | solution.py:218
  18.3 9.6 %all-gather = bf16[8,64,768]{2,1,0:T(8,128)(2,1)S(1)} all-gather(bf16[4,64,768]{2,1,0:T(8,128)(2,1)S(1)} %all_gather.10), channel_id=2, replica_groups={{0,1},{2,3},{4,5},{6,7},{8,9},{10,11},{12,13},{14,15},{16,17},{18,19},{..., dimensions={0}, use_global_device_ids=true | all-gather | bytes 1179648 | tf_op jit(solution)/shard_map/all_gather | solution.py:219
  27.9 0.0 copy-done.8
  27.9 0.0 copy-done
  27.9 0.0 copy-start.1
  27.9 1.2 %copy-done.1 = bf16[256,2048]{1,0:T(8,128)(2,1)S(1)} copy-done((bf16[256,2048]{1,0:T(8,128)(2,1)S(1)}, bf16[256,2048]{1,0:T(8,128)(2,1)}, u32[]{:S(2)}) %copy-start.1) | copy-done | bytes 1048600
  29.2 0.0 copy-start.2
  29.2 0.0 copy-start.3
  29.2 0.0 copy-start.4
  29.2 0.0 copy-start.5
  29.2 0.0 copy-start.6
  29.2 0.0 copy-start.7
  29.2 0.0 copy-start.9
  29.2 3.8 %gradient_terms.1 = bf16[8,400,128]{2,1,0:T(8,128)(2,1)} custom-call(s32[1]{0:T(128)S(6)} %copy.26.length_ref, bf16[256,2048]{1,0:T(8,128)(2,1)S(1)} %copy-done.1, bf16[256,4096]{1,0:T(8,128)(2,1)S(1)} %copy-done, bf16[2,4,64,768]{3,2,1,0:T(8,128)(2,1)S(1)} %bitcast.3, bf16[1,4096]{1,0:T(2,128)(2,1)S(1)} %reshape.47.gain_ref, f32[1,4096]{1,0:T(1,128)S(1)} %bitcast.4), custom_call_target="tpu_custom_call" | custom-call | tf_op jit(solution)/shard_map/gradient_terms/pallas_call | solution.py:232
  33.0 3.8 %all-to-all-start = ((bf16[8,400,128]{2,1,0:T(8,128)(2,1)}), bf16[8,400,128]{2,1,0:T(8,128)(2,1)S(1)}, u32[]{:S(2)}, u32[]{:S(2)}) async-start(bf16[8,400,128]{2,1,0:T(8,128)(2,1)} %gradient_terms.1), calls=%async_computation | async-start | bytes 1638400 | tf_op jit(solution)/shard_map/all_to_all | solution.py:240
  37.5 20.2 %all-to-all-done.terms_ref = bf16[8,400,128]{2,1,0:T(8,128)(2,1)S(1)} async-done(((bf16[8,400,128]{2,1,0:T(8,128)(2,1)}), bf16[8,400,128]{2,1,0:T(8,128)(2,1)S(1)}, u32[]{:S(2)}, u32[]{:S(2)}) %all-to-all-start) | async-done | bytes 819232 | tf_op jit(solution)/shard_map/all_to_all | solution.py:240
  57.7 0.0 copy-done.2
  57.7 0.0 copy-done.3
  57.7 0.0 copy-done.4
  57.7 0.0 copy-done.5
  57.7 0.0 copy-done.6
  57.7 0.0 copy-done.7
  57.7 0.0 copy-done.9
  57.7 1.2 %update.1 = (f32[1,64,256]{2,1,0:T(8,128)S(1)}, f32[1,64,256]{2,1,0:T(8,128)S(1)}, f32[1,64,256]{2,1,0:T(8,128)S(1)}, f32[1,64,512]{2,1,0:T(8,128)S(1)}, f32[1,6...) custom-call(s32[1,8]{1,0:T(1,128)S(1)} %copy-done.9, ...), custom_call_target="tpu_custom_call" | custom-call | tf_op jit(solution)/shard_map/update/pallas_call | solution.py:242
  59.0 34.6 %conditional.1 = (bf16[3,384,128]{2,1,0:T(8,128)(2,1)}) conditional(s32[]{:T(128)} %clamp.3, bf16[3,384,128]{2,1,0:T(8,128)(2,1)S(1)} %get-tuple-element.34, bf16[3,384,128]{2,1,0:T(8,128)(2,1)S(1)} %get-tuple-element.34, bf16[3,384,128]{2,1,0:T(8,128)(2,1)S(1)} %get-tuple-element.34, ...), branch_computations={%region_0.1_spmd, %region_1.2_spmd, %region_2.3_spmd, %region_3.4_... | conditional | bytes 1179696 | solution.py:255
  59.0 9.2 %collective-permute-start.5 = (bf16[3,384,128]{2,1,0:T(8,128)(2,1)S(1)}, bf16[3,384,128]{2,1,0:T(8,128)(2,1)}, u32[]{:S(2)}, u32[]{:S(2)}) collective-permute-start(bf16[3,384,128]{2,1,0:T(8,128)(2,1)S(1)} %param.5), channel_id=1, source_target_pairs={{0,256},{8,264},{16,272},{24,280},{32,288},{40,296},{48,304},{56,3... | collective-permute-start | bytes 884744 | tf_op jit(solution)/shard_map/cond/branch_5_fun/ppermute | solution.py:209
  68.2 25.3 %collective-permute-done.5 = bf16[3,384,128]{2,1,0:T(8,128)(2,1)} collective-permute-done((bf16[3,384,128]{2,1,0:T(8,128)(2,1)S(1)}, bf16[3,384,128]{2,1,0:T(8,128)(2,1)}, u32[]{:S(2)}, u32[]{:S(2)}) %collective-permute-start.5) | collective-permute-done | bytes 294944 | tf_op jit(solution)/shard_map/cond/branch_5_fun/ppermute | solution.py:209
  93.5 1.8 %average.1 = (f32[1,64,256]{2,1,0:T(8,128)}, f32[1,64,256]{2,1,0:T(8,128)}, f32[1,64,256]{2,1,0:T(8,128)}, f32[1,64,512]{2,1,0:T(8,128)}, f32[1,64,512]{2,1,0:T(8,128)}, /*index=5*/f32[1,64,512]{2,1,0:T(8,128)}) custom-call(bf16[3,384,128]{2,1,0:T(8,128)(2,1)} %get-tuple-element.48.theirs_ref, f32[1,64,256]{2,1,0:T(8,128)S(1)} %get-tuple-element.35.refs_0_, ...), custom_call_target="tpu_custom_call" | custom-call | tf_op jit(solution)/shard_map/average/pallas_call | solution.py:256
  (1 shorter events, 0.0 us)
Async XLA Ops:
  0.6 27.3 %copy-start.8 = (f32[4096]{0:T(1024)S(1)}, f32[4096]{0:T(1024)}, u32[]{:S(2)}) copy-start(f32[4096]{0:T(1024)} %param.30) | copy-start | bytes 49156
  0.6 27.3 %copy-start = (bf16[256,4096]{1,0:T(8,128)(2,1)S(1)}, bf16[256,4096]{1,0:T(8,128)(2,1)}, u32[]{:S(2)}) copy-start(bf16[256,4096]{1,0:T(8,128)(2,1)} %r_ref.1) | copy-start | bytes 6291460
  27.9 1.2 %copy-start.1 = (bf16[256,2048]{1,0:T(8,128)(2,1)S(1)}, bf16[256,2048]{1,0:T(8,128)(2,1)}, u32[]{:S(2)}) copy-start(bf16[256,2048]{1,0:T(8,128)(2,1)} %x_ref.1) | copy-start | bytes 3145732
  29.2 28.5 %copy-start.2 = (f32[1,64,512]{2,1,0:T(8,128)S(1)}, f32[1,64,512]{2,1,0:T(8,128)}, u32[]{:S(2)}) copy-start(f32[1,64,512]{2,1,0:T(8,128)} %b_ref.1) | copy-start | bytes 393220
  29.2 28.5 %copy-start.3 = (f32[1,64,256]{2,1,0:T(8,128)S(1)}, f32[1,64,256]{2,1,0:T(8,128)}, u32[]{:S(2)}) copy-start(f32[1,64,256]{2,1,0:T(8,128)} %a_ref.1) | copy-start | bytes 196612
  29.2 28.5 %copy-start.4 = (f32[1,64,512]{2,1,0:T(8,128)S(1)}, f32[1,64,512]{2,1,0:T(8,128)}, u32[]{:S(2)}) copy-start(f32[1,64,512]{2,1,0:T(8,128)} %mb_ref.1) | copy-start | bytes 393220
  29.2 28.5 %copy-start.5 = (f32[1,64,512]{2,1,0:T(8,128)S(1)}, f32[1,64,512]{2,1,0:T(8,128)}, u32[]{:S(2)}) copy-start(f32[1,64,512]{2,1,0:T(8,128)} %vb_ref.1) | copy-start | bytes 393220
  29.2 28.5 %copy-start.6 = (f32[1,64,256]{2,1,0:T(8,128)S(1)}, f32[1,64,256]{2,1,0:T(8,128)}, u32[]{:S(2)}) copy-start(f32[1,64,256]{2,1,0:T(8,128)} %ma_ref.1) | copy-start | bytes 196612
  29.2 28.5 %copy-start.7 = (f32[1,64,256]{2,1,0:T(8,128)S(1)}, f32[1,64,256]{2,1,0:T(8,128)}, u32[]{:S(2)}) copy-start(f32[1,64,256]{2,1,0:T(8,128)} %va_ref.1) | copy-start | bytes 196612
  29.2 28.5 %copy-start.9 = (s32[1,8]{1,0:T(1,128)S(1)}, s32[1,8]{1,0:T(1,128)}, u32[]{:S(2)}) copy-start(s32[1,8]{1,0:T(1,128)} %ranks_ref.1) | copy-start | bytes 100
  33.0 24.7 %all-to-all-start = ((bf16[8,400,128]{2,1,0:T(8,128)(2,1)}), bf16[8,400,128]{2,1,0:T(8,128)(2,1)S(1)}, u32[]{:S(2)}, u32[]{:S(2)}) async-start(bf16[8,400,128]{2,1,0:T(8,128)(2,1)} %gradient_terms.1), calls=%async_computation | async-start | bytes 1638400 | tf_op jit(solution)/shard_map/all_to_all | solution.py:240
  59.0 34.5 %collective-permute-start.5 = (bf16[3,384,128]{2,1,0:T(8,128)(2,1)S(1)}, bf16[3,384,128]{2,1,0:T(8,128)(2,1)}, u32[]{:S(2)}, u32[]{:S(2)}) collective-permute-start(bf16[3,384,128]{2,1,0:T(8,128)(2,1)S(1)} %param.5), channel_id=1, source_target_pairs={{0,256},{8,264},{16,272},{24,280},{32,288},{40,296},{48,304},{56,3... | collective-permute-start | bytes 884744 | tf_op jit(solution)/shard_map/cond/branch_5_fun/ppermute | solution.py:209

commit v2 on v1

v2 whole, which is shorter than its diff:
```python
import jax
import jax.numpy as jnp
import numpy as np
from jax import lax
from jax.experimental import pallas as pl
from jax.experimental.pallas import tpu as pltpu
from jax.sharding import PartitionSpec as P

F32 = jnp.float32
BF16 = jnp.bfloat16
RANK = 64
LANES = 128
TAIL = 16
COUNT_BITS = 10
VMEM = pl.BlockSpec(memory_space=pltpu.VMEM)
SMEM = pl.BlockSpec(memory_space=pltpu.SMEM)


def nt(left, right):
    return lax.dot_general(left, right, (((1,), (1,)), ((), ())), preferred_element_type=F32)


def tn(left, right):
    return lax.dot_general(left, right, (((0,), (0,)), ((), ())), preferred_element_type=F32)


def nn(left, right):
    return lax.dot_general(left, right, (((1,), (0,)), ((), ())), preferred_element_type=F32)


def split_two(value):
    high = value.astype(BF16)
    return high, (value - high.astype(F32)).astype(BF16)


def split_three(value):
    high = value.astype(BF16)
    rest = value - high.astype(F32)
    middle = rest.astype(BF16)
    return high, middle, (rest - middle.astype(F32)).astype(BF16)


def fold_rows(stacked):
    half = stacked.shape[0] // 2
    return stacked[:half] + stacked[half:]


def stage_inputs(x_ref, r_ref, gain_ref, head_ref, x_out_ref, r_out_ref, squares_ref, w_ref, rows_ref):
    x_out_ref[...] = x_ref[...]
    tokens, width = r_ref.shape
    w = gain_ref[...].astype(F32) * head_ref[...]
    w_ref[...] = w
    parts = [part.astype(F32) for part in split_three(w)]
    row = lax.broadcasted_iota(jnp.int32, (TAIL, LANES), 0)
    squares = jnp.zeros((tokens, LANES), F32)
    for c in range(width // LANES):
        cols = slice(c * LANES, (c + 1) * LANES)
        high, middle, low = [part[c : c + 1] for part in parts]
        rows = jnp.where(row == 0, high, jnp.where(row == 1, middle, low))
        rows_ref[:, cols] = jnp.where(row < 3, rows, 0.0).astype(BF16)
        piece = r_ref[:, cols]
        r_out_ref[:, cols] = piece
        squares += piece.astype(F32) * piece.astype(F32)
    squares_ref[...] = jnp.broadcast_to(jnp.sum(squares, axis=1, keepdims=True), (tokens, LANES))


def gradient_terms(length_ref, x_ref, r_ref, weights_ref, squares_ref, w_ref, rows_ref, out_ref):
    shards = out_ref.shape[0]
    tokens, width = r_ref.shape
    down_cols = x_ref.shape[1] // shards
    up_cols = width // shards

    def down(shard):
        return weights_ref[shard % 2, shard // 2, :, :down_cols]

    def up(shard):
        return weights_ref[shard % 2, shard // 2, :, down_cols:]

    z = jnp.zeros((tokens, RANK), F32)
    p_ext = jnp.zeros((tokens, RANK + TAIL), F32)
    gram = jnp.zeros((RANK + TAIL, RANK + TAIL), F32)
    for f in range(shards):
        z += nt(x_ref[:, f * down_cols : (f + 1) * down_cols], down(f))
        cols = slice(f * up_cols, (f + 1) * up_cols)
        b_ext = jnp.concatenate([up(f), rows_ref[:, cols]], axis=0)
        p_ext += nt(r_ref[:, cols], b_ext)
        gram += nt(b_ext, b_ext)
    squares = squares_ref[:, :1]

    z16 = z.astype(BF16)
    zf = z16.astype(F32)
    p = p_ext[:, :RANK]
    m_high, m_middle, m_low = split_three(gram[:RANK, :RANK])
    v = p + (nn(z16, m_high) + (nn(z16, m_middle) + nn(z16, m_low)))
    bw = jnp.sum(gram[RANK : RANK + 3, :RANK], axis=0, keepdims=True)
    rw = jnp.sum(p_ext[:, RANK : RANK + 3], axis=1, keepdims=True)
    total = squares + jnp.sum(zf * (p + v), axis=1, keepdims=True)
    along = rw + jnp.sum(zf * bw, axis=1, keepdims=True)
    scale = lax.rsqrt(total * (1.0 / width) + 1e-05)

    length = length_ref[0]
    token = lax.broadcasted_iota(jnp.int32, (tokens, 1), 0)
    over = jnp.where(token < length, 1.0 / jnp.full((tokens, 1), length, jnp.int32).astype(F32), 0.0)
    score = jnp.sum(over * scale * along, axis=0, keepdims=True)
    alpha = over * scale
    beta = over * scale * scale * scale * along * (1.0 / width)

    dz = jnp.concatenate(split_two(alpha * bw - beta * v), axis=1)
    bz = jnp.concatenate(split_two(beta * zf), axis=1)
    az = jnp.concatenate(split_two(alpha * zf), axis=1)
    az_sum = fold_rows(tn(az, jnp.ones((tokens, LANES), BF16)))
    inner = jnp.concatenate(split_two(fold_rows(tn(bz, z16))), axis=0)
    s_high, s_middle, s_low = split_three(jnp.broadcast_to(score, (TAIL, LANES)))
    tail_row = lax.broadcasted_iota(jnp.int32, (TAIL, LANES), 0)
    tail = jnp.where(
        tail_row == 0,
        s_high.astype(F32),
        jnp.where(tail_row == 1, s_middle.astype(F32), s_low.astype(F32)),
    ).astype(BF16)
    for f in range(shards):
        term_a = fold_rows(tn(dz, x_ref[:, f * down_cols : (f + 1) * down_cols])).astype(BF16)
        at = 0
        for c in range(down_cols // LANES):
            out_ref[f, at : at + RANK, :] = term_a[:, c * LANES : (c + 1) * LANES]
            at += RANK
        term_b = fold_rows(
            tn(bz, r_ref[:, f * up_cols : (f + 1) * up_cols]) + nn(inner, up(f))
        )
        for c in range(up_cols // LANES):
            panel = f * up_cols // LANES + c
            out_ref[f, at : at + RANK, :] = (
                az_sum * w_ref[panel : panel + 1] - term_b[:, c * LANES : (c + 1) * LANES]
            ).astype(BF16)
            at += RANK
        out_ref[f, at : at + TAIL, :] = tail


def power_gap(base, count):
    factor = float(np.float32(base))
    gap = jnp.float32(0.0)
    for bit in range(COUNT_BITS):
        part = jnp.float32(1.0 - factor ** (2**bit))
        gap = jnp.where((count >> bit) & 1 == 1, gap + part - gap * part, gap)
    return gap


def pull_scores(ranks_ref, terms_ref, loss_ref):
    shards = terms_ref.shape[0]
    base = terms_ref.shape[1] - TAIL
    square = (shards, LANES)
    sublane = lax.broadcasted_iota(jnp.int32, square, 0)
    lane = lax.broadcasted_iota(jnp.int32, square, 1)
    score_col = jnp.zeros(square, F32)
    score_row = jnp.zeros(square, F32)
    place_col = jnp.zeros(square, jnp.int32)
    place_row = jnp.zeros(square, jnp.int32)
    for d in range(shards):
        parts = terms_ref[d, base : base + TAIL, :].astype(F32)
        one = jnp.broadcast_to(parts[0:1] + (parts[1:2] + parts[2:3]), square)
        score_col = jnp.where(sublane == d, one, score_col)
        score_row = jnp.where(lane == d, one, score_row)
        place_col = jnp.where(sublane == ranks_ref[0, d], d, place_col)
        place_row = jnp.where(lane == ranks_ref[0, d], d, place_row)
    live = lane < shards
    after = jnp.where(live & (place_col >= place_row), 1.0, 0.0)
    weight = jnp.exp(score_col)
    tails = jnp.where(live[:1], jnp.sum(after * weight, axis=0, keepdims=True), 1.0)
    losses = jnp.where(live[:1], jnp.log(tails) - score_row[:1], 0.0)
    loss_ref[0] = jnp.sum(losses)
    return jnp.sum(after * (weight / tails), axis=1, keepdims=True) - 1.0


def weighed(pull, terms_ref, rows):
    grad = pull[:1] * terms_ref[0, rows, :].astype(F32)
    for d in range(1, terms_ref.shape[0]):
        grad += pull[d : d + 1] * terms_ref[d, rows, :].astype(F32)
    return grad


def adamw(count, grad, param, moment, second):
    one_fix = 1.0 / jnp.full(grad.shape, power_gap(0.9, count), F32)
    two_fix = 1.0 / jnp.full(grad.shape, power_gap(0.999, count), F32)
    moment = 0.9 * moment + 0.1 * grad
    second = 0.999 * second + 0.001 * grad * grad
    change = moment * one_fix / (jnp.sqrt(second * two_fix) + 1e-08) + 0.01 * param
    return param - 0.001 * change, moment, second


def panels_of(refs):
    at = 0
    for first in (0, 3):
        for c in range(refs[first].shape[2] // LANES):
            yield slice(at, at + RANK), first, slice(c * LANES, (c + 1) * LANES)
            at += RANK


def pack_weights(a_ref, b_ref, out_ref):
    cols = a_ref.shape[2]
    for copy in range(out_ref.shape[0]):
        out_ref[copy, :, :cols] = a_ref[0].astype(BF16)
        out_ref[copy, :, cols:] = b_ref[0].astype(BF16)


def pack_state(*refs):
    out_ref = refs[-1]
    for rows, first, cols in panels_of(refs[:6]):
        for i in range(3):
            out_ref[i, rows, :] = refs[first + i][0, :, cols].astype(BF16)


def update(ranks_ref, step_ref, terms_ref, *refs):
    state, out, packed_ref, loss_ref = refs[:6], refs[6:12], refs[12], refs[13]
    pull = pull_scores(ranks_ref, terms_ref, loss_ref)
    for rows, first, cols in panels_of(state):
        grad = weighed(pull, terms_ref, rows)
        old = [state[first + i][0, :, cols] for i in range(3)]
        for i, value in enumerate(adamw(step_ref[0] + 1, grad, *old)):
            out[first + i][0, :, cols] = value
            packed_ref[i, rows, :] = value.astype(BF16)


def average(theirs_ref, *refs):
    mine, out = refs[:6], refs[6:]
    for rows, first, cols in panels_of(mine):
        for i in range(3):
            out[first + i][0, :, cols] = 0.5 * (
                mine[first + i][0, :, cols] + theirs_ref[i, rows, :].astype(F32)
            )


def gradient(ranks_ref, terms_ref, grad_ref, packed_ref, loss_ref):
    pull = pull_scores(ranks_ref, terms_ref, loss_ref)
    for first in range(0, grad_ref.shape[0], RANK):
        rows = slice(first, first + RANK)
        grad = weighed(pull, terms_ref, rows)
        grad_ref[rows, :] = grad
        packed_ref[rows, :] = grad.astype(BF16)


def own_update(step_ref, grad_ref, *refs):
    state, out = refs[:6], refs[6:]
    for rows, first, cols in panels_of(state):
        old = [state[first + i][0, :, cols] for i in range(3)]
        for i, value in enumerate(adamw(step_ref[0] + 1, grad_ref[rows, :], *old)):
            out[first + i][0, :, cols] = value


def their_update(step_ref, grad_ref, state_ref, *refs):
    mine, out = refs[:6], refs[6:]
    for rows, first, cols in panels_of(mine):
        old = [state_ref[i, rows, :].astype(F32) for i in range(3)]
        grad = grad_ref[rows, :].astype(F32)
        for i, value in enumerate(adamw(step_ref[0] + 1, grad, *old)):
            out[first + i][0, :, cols] = 0.5 * (mine[first + i][0, :, cols] + value)


def call(kernel, out_shape, smem, operands, out_specs=None, cost=(0, 0)):
    many = isinstance(out_shape, (list, tuple))
    if out_specs is None:
        out_specs = [VMEM] * len(out_shape) if many else VMEM
    return pl.pallas_call(
        kernel,
        out_shape=out_shape,
        in_specs=[SMEM] * smem + [VMEM] * (len(operands) - smem),
        out_specs=out_specs,
        compiler_params=pltpu.CompilerParams(vmem_limit_bytes=16 * 2**20),
        cost_estimate=pl.CostEstimate(flops=cost[0], bytes_accessed=cost[1], transcendentals=0),
        name=kernel.__name__,
    )(*operands)


def shape(dims, dtype):
    return jax.ShapeDtypeStruct(dims, dtype)


def whole_step(bit, operands):
    (
        features, resid, down_weight, up_weight, down_moment, down_variance, up_moment,
        up_variance, lengths, ranks, gain, head, step,
    ) = operands
    shards = lax.axis_size("fsdp")
    replicas = lax.axis_size("rep")
    swap = [(i, i ^ 1 << bit) for i in range(replicas)]
    cols = down_weight.shape[2] + up_weight.shape[2]
    rows = cols // LANES * RANK
    panels = resid.shape[1] // LANES
    state = (down_weight, down_moment, down_variance, up_weight, up_moment, up_variance)
    kept = [shape(s.shape, F32) for s in state]
    loss_shape = shape((1,), F32)
    same_core = [list(range(core, shards, 2)) for core in range(2)]
    same_chip = [[first, first + 1] for first in range(0, shards, 2)]
    packed = call(
        pack_weights, shape((shards // 2, RANK, cols), BF16), 0, (down_weight, up_weight)
    )
    across = lax.all_to_all(packed, "fsdp", 0, 0, axis_index_groups=same_core)
    tokens, width = resid.shape
    features, resid, squares, w, w_rows = call(
        stage_inputs,
        [
            shape(features.shape, BF16), shape(resid.shape, BF16), shape((tokens, LANES), F32),
            shape((panels, LANES), F32), shape((TAIL, width), BF16),
        ],
        0,
        (features, resid, gain.reshape(panels, LANES), head.reshape(panels, LANES)),
        cost=(tokens * width * 4, tokens * width * 6),
    )
    weights = lax.all_gather(across, "fsdp", axis_index_groups=same_chip)
    terms = call(
        gradient_terms,
        shape((shards, rows + TAIL, LANES), BF16),
        1,
        (lengths, features, resid, weights, squares, w, w_rows),
    )
    terms = lax.all_to_all(terms, "fsdp", 0, 0)
    if replicas >> bit <= 4:
        *mine, packed, loss = call(
            update,
            kept + [shape((3, rows, LANES), BF16), loss_shape],
            2,
            (ranks, step, terms) + state,
            [VMEM] * 7 + [SMEM],
        )
        theirs = lax.ppermute(packed, "rep", swap)
        mixed = call(average, kept, 0, (theirs,) + tuple(mine))
    else:
        old = call(pack_state, shape((3, rows, LANES), BF16), 0, state)
        their_state = lax.ppermute(old, "rep", swap)
        grad, grad16, loss = call(
            gradient,
            [shape((rows, LANES), F32), shape((rows, LANES), BF16), loss_shape],
            1,
            (ranks, terms),
            [VMEM, VMEM, SMEM],
        )
        their_grad = lax.ppermute(grad16, "rep", swap)
        mine = call(
            own_update, kept, 1, (step, grad) + state, cost=(rows * LANES * 40, rows * LANES * 24)
        )
        mixed = call(their_update, kept, 1, (step, their_grad, their_state) + tuple(mine))
    new_a, new_ma, new_va, new_b, new_mb, new_vb = mixed
    return new_a, new_b, new_ma, new_va, new_mb, new_vb, loss


def with_bit(bit):

    def step(operands):
        return whole_step(bit, operands)

    return step


def per_device(*operands):
    levels = lax.axis_size("rep").bit_length() - 1
    step = operands[-1]
    return lax.switch(step[0] % levels, [with_bit(bit) for bit in range(levels)], operands)


def solution(mesh):
    rows = P(("rep", "fsdp"), None)
    cols = P("rep", None, "fsdp")
    in_specs = (rows, rows) + (cols,) * 6 + (P(("rep", "fsdp")), P("rep", None), P(), P(), P())
    out_specs = (cols,) * 6 + (P("rep"),)
    return jax.shard_map(
        per_device, mesh=mesh, in_specs=in_specs, out_specs=out_specs, check_vma=False
    )
```

time: 95.7 us -> 64.7 us (0.68)
  waiting for transfers between devices: 45.5 us -> 22.8 us
  blocking collectives: 24 us -> 7.84 us
  Pallas kernels: 6.84 us -> 13.4 us
  starting transfers between devices: 13.1 us -> 18.6 us
  local copies, waits for them, and re-layouts: 1.98 us -> 0.03 us
  other arithmetic: 1.77 us -> 0 us
    ppermute x1 -> x2, waiting for transfers between devices: 25.3 us -> 1.89 us  [the longest x1 1.89 us: whole_step(): their_grad = lax.ppermute(grad16, 'rep', swap)]
    all_gather x2 -> x1, blocking collectives: 24 us -> 7.84 us  [whole_step(): weights = lax.all_gather(across, 'fsdp', axis_index_groups=same_chip)]
    all_to_all x1 -> x2, starting transfers between devices: 3.82 us -> 10.4 us  [the longest x1 6.44 us: whole_step(): across = lax.all_to_all(packed, 'fsdp', 0, 0, axis_index_groups=same_core)]
    pallas_call x3 -> x7, Pallas kernels: 6.84 us -> 13.4 us  [call(): pl.pallas_call(kernel, out_shape=out_shape, in_specs=[SMEM] * smem + [VME...]
    another operation x2 -> x0, other arithmetic: 1.76 us -> none
    unnamed x20 -> x0, local copies, waits for them, and re-layouts: 1.27 us -> none
    ppermute x1 -> x2, starting transfers between devices: 9.24 us -> 8.16 us  [the longest x1 4.08 us: whole_step(): their_state = lax.ppermute(old, 'rep', swap)]
    all_to_all x1 -> x2, waiting for transfers between devices: 20.2 us -> 21 us  [the longest x1 15.6 us: whole_step(): terms = lax.all_to_all(terms, 'fsdp', 0, 0)]
  transfers between devices with their start and end apart: 2 -> 4, of which waited for: 2 -> 3; matrix products, arithmetic and copies ran while one was open for 0% -> 0% of each run, Pallas kernels for 0% -> 9%
where the time goes in v2:
time: 64.7 us; the launch traced here: 64.3 us
  waiting for transfers between devices  22.8 us (35%)
  starting transfers between devices  18.6 us (29%)
  Pallas kernels  13.4 us (21%)
  blocking collectives  7.84 us (12%)
  between operations  1.3 us (2%)
    all_to_all x1, waiting for transfers between devices, whole_step(): terms = lax.all_to_all(terms, 'fsdp', 0, 0)  15.6 us
    pallas_call x7, Pallas kernels, call(): pl.pallas_call(kernel, out_shape=out_shape, in_specs=[SMEM] * smem + [VME...  13.4 us
    all_gather x1, blocking collectives, whole_step(): weights = lax.all_gather(across, 'fsdp', axis_index_groups=same_chip)  7.84 us
    all_to_all x1, starting transfers between devices, whole_step(): across = lax.all_to_all(packed, 'fsdp', 0, 0, axis_index_groups=same_core)  6.44 us
    all_to_all x1, waiting for transfers between devices, whole_step(): across = lax.all_to_all(packed, 'fsdp', 0, 0, axis_index_groups=same_core)  5.32 us
    ppermute x1, starting transfers between devices, whole_step(): their_state = lax.ppermute(old, 'rep', swap)  4.08 us
    ppermute x1, starting transfers between devices, whole_step(): their_grad = lax.ppermute(grad16, 'rep', swap)  4.08 us
    all_to_all x1, starting transfers between devices, whole_step(): terms = lax.all_to_all(terms, 'fsdp', 0, 0)  3.97 us
  transfers between devices with their start and end apart: 4, of which 3 were waited for; matrix products, arithmetic and copies ran while one was open for 0% of the time, Pallas kernels for 9%

profile of v2, /device:TPU:1, one launch (start us, length us, event | category | flops | bytes accessed | tf_op | source)
XLA Modules:
  0.0 64.3 jit_solution(11112147203152275874)
XLA Ops:
  1.3 63.0 %conditional.1 = (f32[1,64,256]{2,1,0:T(8,128)}, f32[1,64,512]{2,1,0:T(8,128)}, f32[1,64,256]{2,1,0:T(8,128)}, f32[1,64,256]{2,1,0:T(8,128)}, f32[1,64,512]{2,1,...) conditional(s32[]{:T(128)} %clamp.3, (bf16[4096]{0:T(1024)(128)(2,1)}, ...), branch_computations={%region_0.1_spmd, %region_1.2_spmd, %region_2.3_spmd, %region_3.4_... | conditional | flops 6160384 | bytes 16220684 | solution.py:355
  1.5 1.7 %pack_weights.9 = bf16[4,64,768]{2,1,0:T(8,128)(2,1)} custom-call(f32[1,64,256]{2,1,0:T(8,128)} %get-tuple-element.264.a_ref.refs_0_, f32[1,64,512]{2,1,0:T(8,128)} %get-tuple-element.265.b_ref.refs_3_), custom_call_target="tpu_custom_call" | custom-call | tf_op jit(solution)/shard_map/cond/branch_3_fun/pack_weights/pallas_call | solution.py:261
  3.2 6.4 %all-to-all-start.6 = ((bf16[4,64,768]{2,1,0:T(8,128)(2,1)}), bf16[4,64,768]{2,1,0:T(8,128)(2,1)}, u32[]{:S(2)}, u32[]{:S(2)}) async-start(bf16[4,64,768]{2,1,0:T(8,128)(2,1)} %pack_weights.9), calls=%async_computation.6 | async-start | bytes 786432 | tf_op jit(solution)/shard_map/cond/branch_3_fun/all_to_all | solution.py:295
  9.7 2.5 %stage_inputs.9 = (bf16[256,2048]{1,0:T(8,128)(2,1)S(1)}, bf16[256,4096]{1,0:T(8,128)(2,1)S(1)}, f32[256,128]{1,0:T(8,128)S(1)}, f32[32,128]{1,0:T(8,128)S(1)}, bf16[16,4096]{1,0:T(8,128)(2,1)S(1)}) custom-call(bf16[256,2048]{1,0:T(8,128)(2,1)} %get-tuple-element.258.x_ref, bf16[256,4096]{1,0:T(8,128)(2,1)} %get-tuple-element.259.r_ref, ...), custom_call_target="tpu_custom_call" | custom-call | flops 4194304 | bytes 6291456 | tf_op jit(solution)/shard_map/cond/branch_3_fun/stage_inputs/pallas_call | solution.py:261
  12.2 5.3 %all-to-all-done.6 = bf16[4,64,768]{2,1,0:T(8,128)(2,1)} async-done(((bf16[4,64,768]{2,1,0:T(8,128)(2,1)}), bf16[4,64,768]{2,1,0:T(8,128)(2,1)}, u32[]{:S(2)}, u32[]{:S(2)}) %all-to-all-start.6) | async-done | bytes 393248 | tf_op jit(solution)/shard_map/cond/branch_3_fun/all_to_all | solution.py:295
  17.5 7.8 %all-gather.3 = bf16[8,64,768]{2,1,0:T(8,128)(2,1)S(1)} all-gather(bf16[4,64,768]{2,1,0:T(8,128)(2,1)} %all-to-all-done.6), channel_id=5, replica_groups={{0,1},{2,3},{4,5},{6,7},{8,9},{10,11},{12,13},{14,15},{16,17},{18,19},{..., dimensions={0}, use_global_device_ids=true | all-gather | bytes 1179648 | tf_op jit(solution)/shard_map/cond/branch_3_fun/all_gather | solution.py:307
  25.4 0.0 copy-start.3
  25.4 4.4 %gradient_terms.9 = bf16[8,400,128]{2,1,0:T(8,128)(2,1)} custom-call(s32[1]{0:T(128)} %get-tuple-element.257.length_ref, bf16[256,2048]{1,0:T(8,128)(2,1)S(1)} %get-tuple-element.262.x_ref, bf16[256,4096]{1,0:T(8,128)(2,1)S(1)} %get-tuple-element.263.r_ref, bf16[2,4,64,768]{3,2,1,0:T(8,128)(2,1)S(1)} %bitcast.22, ...), custom_call_target="tpu_custom_call" | custom-call | tf_op jit(solution)/shard_map/cond/branch_3_fun/gradient_terms/pallas_call | solution.py:261
  29.8 0.0 copy-start.39
  29.8 0.0 copy-start.9
  29.8 0.0 copy-start.15
  29.8 0.0 copy-start.21
  29.8 0.0 copy-start.27
  29.8 0.0 copy-start.33
  29.8 4.0 %all-to-all-start.7 = ((bf16[8,400,128]{2,1,0:T(8,128)(2,1)}), bf16[8,400,128]{2,1,0:T(8,128)(2,1)S(1)}, u32[]{:S(2)}, u32[]{:S(2)}) async-start(bf16[8,400,128]{2,1,0:T(8,128)(2,1)} %gradient_terms.9), calls=%async_computation.7 | async-start | bytes 1638400 | tf_op jit(solution)/shard_map/cond/branch_3_fun/all_to_all | solution.py:314
  33.8 0.0 copy-done.3
  33.8 1.1 %pack_state.7 = bf16[3,384,128]{2,1,0:T(8,128)(2,1)S(1)} custom-call(f32[1,64,256]{2,1,0:T(8,128)} %get-tuple-element.264.a_ref.refs_0_, f32[1,64,256]{2,1,0:T(8,128)} %get-tuple-element.270.refs_1_, f32[1,64,256]{2,1,0:T(8,128)} %get-tuple-element.271.refs_2_, f32[1,64,512]{2,1,0:T(8,128)S(1)} %copy-done.3, f32[1,64,512]{2,1,0:T(8,128)} %get-tuple-element.272.refs_4_, ...), custom_call_target="tpu_custom_call" | custom-call | tf_op jit(solution)/shard_map/cond/branch_3_fun/pack_state/pallas_call | solution.py:261
  34.9 4.1 %collective-permute-start.7 = (bf16[3,384,128]{2,1,0:T(8,128)(2,1)S(1)}, bf16[3,384,128]{2,1,0:T(8,128)(2,1)S(1)}, u32[]{:S(2)}, u32[]{:S(2)}) collective-permute-start(bf16[3,384,128]{2,1,0:T(8,128)(2,1)S(1)} %pack_state.7), channel_id=1, source_target_pairs={{0,64},{8,72},{16,80},{24,88},{32,96},{40,104},{48,112},{56,120},{... | collective-permute-start | bytes 884744 | tf_op jit(solution)/shard_map/cond/branch_3_fun/ppermute | solution.py:327
  39.0 15.6 %all-to-all-done.7.terms_ref = bf16[8,400,128]{2,1,0:T(8,128)(2,1)S(1)} async-done(((bf16[8,400,128]{2,1,0:T(8,128)(2,1)}), bf16[8,400,128]{2,1,0:T(8,128)(2,1)S(1)}, u32[]{:S(2)}, u32[]{:S(2)}) %all-to-all-start.7) | async-done | bytes 819232 | tf_op jit(solution)/shard_map/cond/branch_3_fun/all_to_all | solution.py:314
  54.6 0.0 copy-done.39
  54.6 1.2 %gradient.7 = (f32[384,128]{1,0:T(8,128)S(1)}, bf16[384,128]{1,0:T(8,128)(2,1)S(1)}, f32[1]{0:T(128)}) custom-call(s32[1,8]{1,0:T(1,128)S(1)} %copy-done.39, bf16[8,400,128]{2,1,0:T(8,128)(2,1)S(1)} %all-to-all-done.7.terms_ref), custom_call_target="tpu_custom_call" | custom-call | tf_op jit(solution)/shard_map/cond/branch_3_fun/gradient/pallas_call | solution.py:261
  55.8 4.1 %collective-permute-start.6 = (bf16[384,128]{1,0:T(8,128)(2,1)S(1)}, bf16[384,128]{1,0:T(8,128)(2,1)S(1)}, u32[]{:S(2)}, u32[]{:S(2)}) collective-permute-start(bf16[384,128]{1,0:T(8,128)(2,1)S(1)} %get-tuple-element.269), channel_id=1, source_target_pairs={{0,64},{8,72},{16,80},{24,88},{32,96},{40,104},{48,112},{56,120},{... | collective-permute-start | bytes 294920 | tf_op jit(solution)/shard_map/cond/branch_3_fun/ppermute | solution.py:335
  59.9 0.0 copy-done.9
  59.9 0.0 copy-done.15
  59.9 0.0 copy-done.21
  59.9 0.0 copy-done.27
  59.9 0.0 copy-done.33
  60.0 0.8 %own_update.7 = (f32[1,64,256]{2,1,0:T(8,128)S(1)}, f32[1,64,256]{2,1,0:T(8,128)S(1)}, f32[1,64,256]{2,1,0:T(8,128)S(1)}, f32[1,64,512]{2,1,0:T(8,128)S(1)}, f32...) custom-call(s32[1]{0:T(128)} %get-tuple-element.255.step_ref, f32[384,128]{1,0:T(8,128)S(1)} %get-tuple-element.274.grad_ref, ...), custom_call_target="tpu_custom_call" | custom-call | flops 1966080 | bytes 1179648 | tf_op jit(solution)/shard_map/cond/branch_3_fun/own_update/pallas_call | solution.py:261
  60.8 0.0 collective-permute-done.7.state_ref
  60.8 1.9 %collective-permute-done.6.grad_ref = bf16[384,128]{1,0:T(8,128)(2,1)S(1)} collective-permute-done((bf16[384,128]{1,0:T(8,128)(2,1)S(1)}, bf16[384,128]{1,0:T(8,128)(2,1)S(1)}, u32[]{:S(2)}, u32[]{:S(2)}) %collective-permute-start.6) | collective-permute-done | bytes 98336 | tf_op jit(solution)/shard_map/cond/branch_3_fun/ppermute | solution.py:335
  62.7 1.6 %their_update.7 = (f32[1,64,256]{2,1,0:T(8,128)}, f32[1,64,256]{2,1,0:T(8,128)}, f32[1,64,256]{2,1,0:T(8,128)}, f32[1,64,512]{2,1,0:T(8,128)}, f32[1,64,512]{2,1,0:T(8,128)}, /*index=5*/f32[1,64,512]{2,1,0:T(8,128)}) custom-call(s32[1]{0:T(128)} %get-tuple-element.255.step_ref, bf16[384,128]{1,0:T(8,128)(2,1)S(1)} %collective-permute-done.6.grad_ref, ...), custom_call_target="tpu_custom_call" | custom-call | tf_op jit(solution)/shard_map/cond/branch_3_fun/their_update/pallas_call | solution.py:261
Async XLA Ops:
  3.2 14.3 %all-to-all-start.6 = ((bf16[4,64,768]{2,1,0:T(8,128)(2,1)}), bf16[4,64,768]{2,1,0:T(8,128)(2,1)}, u32[]{:S(2)}, u32[]{:S(2)}) async-start(bf16[4,64,768]{2,1,0:T(8,128)(2,1)} %pack_weights.9), calls=%async_computation.6 | async-start | bytes 786432 | tf_op jit(solution)/shard_map/cond/branch_3_fun/all_to_all | solution.py:295
  25.4 8.4 %copy-start.3 = (f32[1,64,512]{2,1,0:T(8,128)S(1)}, f32[1,64,512]{2,1,0:T(8,128)}, u32[]{:S(2)}) copy-start(f32[1,64,512]{2,1,0:T(8,128)} %get-tuple-element.265.b_ref.refs_3_) | copy-start | bytes 393220 | tf_op jit(solution)/shard_map/cond
  29.8 24.8 %copy-start.39 = (s32[1,8]{1,0:T(1,128)S(1)}, s32[1,8]{1,0:T(1,128)}, u32[]{:S(2)}) copy-start(s32[1,8]{1,0:T(1,128)} %get-tuple-element.256.ranks_ref) | copy-start | bytes 100 | tf_op jit(solution)/shard_map/cond
  29.8 30.1 %copy-start.9 = (f32[1,64,256]{2,1,0:T(8,128)S(1)}, f32[1,64,256]{2,1,0:T(8,128)}, u32[]{:S(2)}) copy-start(f32[1,64,256]{2,1,0:T(8,128)} %get-tuple-element.264.a_ref.refs_0_) | copy-start | bytes 196612 | tf_op jit(solution)/shard_map/cond
  29.8 30.2 %copy-start.15 = (f32[1,64,512]{2,1,0:T(8,128)S(1)}, f32[1,64,512]{2,1,0:T(8,128)}, u32[]{:S(2)}) copy-start(f32[1,64,512]{2,1,0:T(8,128)} %get-tuple-element.272.refs_4_) | copy-start | bytes 393220 | tf_op jit(solution)/shard_map/cond
  29.8 30.2 %copy-start.21 = (f32[1,64,512]{2,1,0:T(8,128)S(1)}, f32[1,64,512]{2,1,0:T(8,128)}, u32[]{:S(2)}) copy-start(f32[1,64,512]{2,1,0:T(8,128)} %get-tuple-element.273.refs_5_) | copy-start | bytes 393220 | tf_op jit(solution)/shard_map/cond
  29.8 30.2 %copy-start.27 = (f32[1,64,256]{2,1,0:T(8,128)S(1)}, f32[1,64,256]{2,1,0:T(8,128)}, u32[]{:S(2)}) copy-start(f32[1,64,256]{2,1,0:T(8,128)} %get-tuple-element.270.refs_1_) | copy-start | bytes 196612 | tf_op jit(solution)/shard_map/cond
  29.8 30.2 %copy-start.33 = (f32[1,64,256]{2,1,0:T(8,128)S(1)}, f32[1,64,256]{2,1,0:T(8,128)}, u32[]{:S(2)}) copy-start(f32[1,64,256]{2,1,0:T(8,128)} %get-tuple-element.271.refs_2_) | copy-start | bytes 196612 | tf_op jit(solution)/shard_map/cond
  29.8 24.8 %all-to-all-start.7 = ((bf16[8,400,128]{2,1,0:T(8,128)(2,1)}), bf16[8,400,128]{2,1,0:T(8,128)(2,1)S(1)}, u32[]{:S(2)}, u32[]{:S(2)}) async-start(bf16[8,400,128]{2,1,0:T(8,128)(2,1)} %gradient_terms.9), calls=%async_computation.7 | async-start | bytes 1638400 | tf_op jit(solution)/shard_map/cond/branch_3_fun/all_to_all | solution.py:314
  34.9 25.9 %collective-permute-start.7 = (bf16[3,384,128]{2,1,0:T(8,128)(2,1)S(1)}, bf16[3,384,128]{2,1,0:T(8,128)(2,1)S(1)}, u32[]{:S(2)}, u32[]{:S(2)}) collective-permute-start(bf16[3,384,128]{2,1,0:T(8,128)(2,1)S(1)} %pack_state.7), channel_id=1, source_target_pairs={{0,64},{8,72},{16,80},{24,88},{32,96},{40,104},{48,112},{56,120},{... | collective-permute-start | bytes 884744 | tf_op jit(solution)/shard_map/cond/branch_3_fun/ppermute | solution.py:327
  55.8 6.9 %collective-permute-start.6 = (bf16[384,128]{1,0:T(8,128)(2,1)S(1)}, bf16[384,128]{1,0:T(8,128)(2,1)S(1)}, u32[]{:S(2)}, u32[]{:S(2)}) collective-permute-start(bf16[384,128]{1,0:T(8,128)(2,1)S(1)} %get-tuple-element.269), channel_id=1, source_target_pairs={{0,64},{8,72},{16,80},{24,88},{32,96},{40,104},{48,112},{56,120},{... | collective-permute-start | bytes 294920 | tf_op jit(solution)/shard_map/cond/branch_3_fun/ppermute | solution.py:335

commit v3 on v2

--- a/solution.py
+++ b/solution.py
@@ -12,6 +12,7 @@
 LANES = 128
 TAIL = 16
 COUNT_BITS = 10
+FAR = 2
 VMEM = pl.BlockSpec(memory_space=pltpu.VMEM)
 SMEM = pl.BlockSpec(memory_space=pltpu.SMEM)
 
@@ -45,8 +46,7 @@
     return stacked[:half] + stacked[half:]
 
 
-def stage_inputs(x_ref, r_ref, gain_ref, head_ref, x_out_ref, r_out_ref, squares_ref, w_ref, rows_ref):
-    x_out_ref[...] = x_ref[...]
+def prepare(r_ref, gain_ref, head_ref, squares_ref, w_ref, rows_ref):
     tokens, width = r_ref.shape
     w = gain_ref[...].astype(F32) * head_ref[...]
     w_ref[...] = w
@@ -58,9 +58,8 @@
         high, middle, low = [part[c : c + 1] for part in parts]
         rows = jnp.where(row == 0, high, jnp.where(row == 1, middle, low))
         rows_ref[:, cols] = jnp.where(row < 3, rows, 0.0).astype(BF16)
-        piece = r_ref[:, cols]
-        r_out_ref[:, cols] = piece
-        squares += piece.astype(F32) * piece.astype(F32)
+        piece = r_ref[:, cols].astype(F32)
+        squares += piece * piece
     squares_ref[...] = jnp.broadcast_to(jnp.sum(squares, axis=1, keepdims=True), (tokens, LANES))
 
 
@@ -273,46 +272,15 @@
     return jax.ShapeDtypeStruct(dims, dtype)
 
 
-def whole_step(bit, operands):
-    (
-        features, resid, down_weight, up_weight, down_moment, down_variance, up_moment,
-        up_variance, lengths, ranks, gain, head, step,
-    ) = operands
-    shards = lax.axis_size("fsdp")
+def finish(bit, operands):
+    terms, state, ranks, step = operands
     replicas = lax.axis_size("rep")
     swap = [(i, i ^ 1 << bit) for i in range(replicas)]
-    cols = down_weight.shape[2] + up_weight.shape[2]
-    rows = cols // LANES * RANK
-    panels = resid.shape[1] // LANES
-    state = (down_weight, down_moment, down_variance, up_weight, up_moment, up_variance)
+    rows = terms.shape[1] - TAIL
     kept = [shape(s.shape, F32) for s in state]
     loss_shape = shape((1,), F32)
-    same_core = [list(range(core, shards, 2)) for core in range(2)]
-    same_chip = [[first, first + 1] for first in range(0, shards, 2)]
-    packed = call(
-        pack_weights, shape((shards // 2, RANK, cols), BF16), 0, (down_weight, up_weight)
-    )
-    across = lax.all_to_all(packed, "fsdp", 0, 0, axis_index_groups=same_core)
-    tokens, width = resid.shape
-    features, resid, squares, w, w_rows = call(
-        stage_inputs,
-        [
-            shape(features.shape, BF16), shape(resid.shape, BF16), shape((tokens, LANES), F32),
-            shape((panels, LANES), F32), shape((TAIL, width), BF16),
-        ],
-        0,
-        (features, resid, gain.reshape(panels, LANES), head.reshape(panels, LANES)),
-        cost=(tokens * width * 4, tokens * width * 6),
-    )
-    weights = lax.all_gather(across, "fsdp", axis_index_groups=same_chip)
-    terms = call(
-        gradient_terms,
-        shape((shards, rows + TAIL, LANES), BF16),
-        1,
-        (lengths, features, resid, weights, squares, w, w_rows),
-    )
     terms = lax.all_to_all(terms, "fsdp", 0, 0)
-    if replicas >> bit <= 4:
+    if replicas >> bit <= FAR:
         *mine, packed, loss = call(
             update,
             kept + [shape((3, rows, LANES), BF16), loss_shape],
@@ -344,15 +312,45 @@
 def with_bit(bit):
 
     def step(operands):
-        return whole_step(bit, operands)
+        return finish(bit, operands)
 
     return step
 
 
-def per_device(*operands):
+def per_device(
+    features, resid, down_weight, up_weight, down_moment, down_variance, up_moment, up_variance,
+    lengths, ranks, gain, head, step,
+):
+    shards = lax.axis_size("fsdp")
     levels = lax.axis_size("rep").bit_length() - 1
-    step = operands[-1]
-    return lax.switch(step[0] % levels, [with_bit(bit) for bit in range(levels)], operands)
+    cols = down_weight.shape[2] + up_weight.shape[2]
+    rows = cols // LANES * RANK
+    panels = resid.shape[1] // LANES
+    state = (down_weight, down_moment, down_variance, up_weight, up_moment, up_variance)
+    same_core = [list(range(core, shards, 2)) for core in range(2)]
+    same_chip = [[first, first + 1] for first in range(0, shards, 2)]
+    packed = call(
+        pack_weights, shape((shards // 2, RANK, cols), BF16), 0, (down_weight, up_weight)
+    )
+    across = lax.all_to_all(packed, "fsdp", 0, 0, axis_index_groups=same_core)
+    tokens, width = resid.shape
+    squares, w, w_rows = call(
+        prepare,
+        [shape((tokens, LANES), F32), shape((panels, LANES), F32), shape((TAIL, width), BF16)],
+        0,
+        (resid, gain.reshape(panels, LANES), head.reshape(panels, LANES)),
+        cost=(tokens * width * 4, tokens * width * 6),
+    )
+    weights = lax.all_gather(across, "fsdp", axis_index_groups=same_chip)
+    terms = call(
+        gradient_terms,
+        shape((shards, rows + TAIL, LANES), BF16),
+        1,
+        (lengths, features, resid, weights, squares, w, w_rows),
+    )
+    return lax.switch(
+        step[0] % levels, [with_bit(bit) for bit in range(levels)], (terms, state, ranks, step)
+    )
 
 
 def solution(mesh):

time: 64.7 us -> 92.5 us (1.43)
  the two profiles are of different devices: /device:TPU:1 before, /device:TPU:40 now
where the time goes in v3:
time: 92.5 us; the launch traced here: 92 us
  waiting for transfers between devices  28.9 us (31%)
  blocking collectives  28.7 us (31%)
  starting transfers between devices  20.2 us (22%)
  Pallas kernels  9.25 us (10%)
  local copies, waits for them, and re-layouts  3.01 us (3%)
  between operations  1.97 us (2%)
    all_to_all x1, blocking collectives, finish(): terms = lax.all_to_all(terms, 'fsdp', 0, 0)  26.1 us
    ppermute x1, waiting for transfers between devices, finish(): theirs = lax.ppermute(packed, 'rep', swap)  24.4 us
    ppermute x1, starting transfers between devices, finish(): theirs = lax.ppermute(packed, 'rep', swap)  14.2 us
    pallas_call x5, Pallas kernels, call(): pl.pallas_call(kernel, out_shape=out_shape, in_specs=[SMEM] * smem + [VME...  9.25 us
    all_to_all x1, starting transfers between devices, per_device(): across = lax.all_to_all(packed, 'fsdp', 0, 0, axis_index_groups=same_core)  6 us
    all_to_all x1, waiting for transfers between devices, per_device(): across = lax.all_to_all(packed, 'fsdp', 0, 0, axis_index_groups=same_core)  4.45 us
    unnamed x12, local copies, waits for them, and re-layouts  3.01 us
    all_gather x1, blocking collectives, per_device(): weights = lax.all_gather(across, 'fsdp', axis_index_groups=same_chip)  2.57 us
  transfers between devices with their start and end apart: 2, of which 2 were waited for; matrix products, arithmetic and copies ran while one was open for 0% of the time, Pallas kernels for 1%

profile of v3, /device:TPU:40, one launch (start us, length us, event | category | flops | bytes accessed | tf_op | source)
XLA Modules:
  0.0 92.0 jit_solution(8343763123475658853)
XLA Ops:
  0.6 0.0 copy-start.2
  0.6 1.8 %pack_weights.1 = bf16[4,64,768]{2,1,0:T(8,128)(2,1)} custom-call(f32[1,64,256]{2,1,0:T(8,128)} %a_ref.1, f32[1,64,512]{2,1,0:T(8,128)} %b_ref.1), custom_call_target="tpu_custom_call" | custom-call | tf_op jit(solution)/shard_map/pack_weights/pallas_call | solution.py:260
  2.4 6.0 %all-to-all-start.6 = ((bf16[4,64,768]{2,1,0:T(8,128)(2,1)}), bf16[4,64,768]{2,1,0:T(8,128)(2,1)}, u32[]{:S(2)}, u32[]{:S(2)}) async-start(bf16[4,64,768]{2,1,0:T(8,128)(2,1)} %pack_weights.1), calls=%async_computation.6 | async-start | bytes 786432 | tf_op jit(solution)/shard_map/all_to_all | solution.py:335
  9.8 0.0 copy-start
  9.8 1.6 %copy-done = bf16[256,4096]{1,0:T(8,128)(2,1)S(1)} copy-done((bf16[256,4096]{1,0:T(8,128)(2,1)S(1)}, bf16[256,4096]{1,0:T(8,128)(2,1)}, u32[]{:S(2)}) %copy-start) | copy-done | bytes 2097176
  11.3 0.0 copy-start.3
  11.3 0.7 copy-done.3
  12.1 0.0 copy-start.4
  12.1 0.7 copy-done.4
  12.8 0.0 copy-start.1
  12.8 0.5 prepare.1
  13.3 4.4 %all-to-all-done.6 = bf16[4,64,768]{2,1,0:T(8,128)(2,1)} async-done(((bf16[4,64,768]{2,1,0:T(8,128)(2,1)}), bf16[4,64,768]{2,1,0:T(8,128)(2,1)}, u32[]{:S(2)}, u32[]{:S(2)}) %all-to-all-start.6) | async-done | bytes 393248 | tf_op jit(solution)/shard_map/all_to_all | solution.py:335
  17.7 2.6 %all-gather = bf16[8,64,768]{2,1,0:T(8,128)(2,1)S(1)} all-gather(bf16[4,64,768]{2,1,0:T(8,128)(2,1)} %all-to-all-done.6), channel_id=2, replica_groups={{0,1},{2,3},{4,5},{6,7},{8,9},{10,11},{12,13},{14,15},{16,17},{18,19},{..., dimensions={0}, use_global_device_ids=true | all-gather | bytes 1179648 | tf_op jit(solution)/shard_map/all_gather | solution.py:344
  20.3 0.0 copy-done.2
  20.3 0.0 copy-done.1
  20.3 0.0 copy-start.5
  20.3 3.7 %gradient_terms.1 = bf16[8,400,128]{2,1,0:T(8,128)(2,1)} custom-call(s32[1]{0:T(128)S(6)} %copy.62.length_ref, bf16[256,2048]{1,0:T(8,128)(2,1)S(1)} %copy-done.2, bf16[256,4096]{1,0:T(8,128)(2,1)S(1)} %copy-done.1, bf16[2,4,64,768]{3,2,1,0:T(8,128)(2,1)S(1)} %bitcast.4, f32[256,128]{1,0:T(8,128)S(1)} %get-tuple-element.261.squares_ref, ...), custom_call_target="tpu_custom_call" | custom-call | tf_op jit(solution)/shard_map/gradient_terms/pallas_call | solution.py:260
  24.0 0.0 copy-done.5
  24.0 68.0 %conditional.1 = (f32[1,64,256]{2,1,0:T(8,128)}, f32[1,64,512]{2,1,0:T(8,128)}, f32[1,64,256]{2,1,0:T(8,128)}, f32[1,64,256]{2,1,0:T(8,128)}, f32[1,64,512]{2,1,...) conditional(s32[]{:T(128)} %clamp.3, (bf16[8,400,128]{2,1,0:T(8,128)(2,1)}, ...), branch_computations={%region_0.1_spmd, %region_1.2_spmd, %region_2.3_spmd, %region_3.4_... | conditional | flops 1966080 | bytes 7045584 | solution.py:351
  24.0 26.1 %all_to_all.29.terms_ref = bf16[8,400,128]{2,1,0:T(8,128)(2,1)S(1)} all-to-all(bf16[8,400,128]{2,1,0:T(8,128)(2,1)} %get-tuple-element.230), channel_id=1, replica_groups=mesh['rep'=64,'fsdp'=8] {'fsdp'}, dimensions={0} | all-to-all | bytes 1638400 | tf_op jit(solution)/shard_map/cond/branch_5_fun/all_to_all | solution.py:282
  50.1 2.4 %update.1 = (f32[1,64,256]{2,1,0:T(8,128)S(1)}, f32[1,64,256]{2,1,0:T(8,128)S(1)}, f32[1,64,256]{2,1,0:T(8,128)S(1)}, f32[1,64,512]{2,1,0:T(8,128)S(1)}, f32[1,6...) custom-call(s32[1,8]{1,0:T(1,128)} %get-tuple-element.228.ranks_ref, ...), custom_call_target="tpu_custom_call" | custom-call | tf_op jit(solution)/shard_map/cond/branch_5_fun/update/pallas_call | solution.py:260
  52.5 14.2 %collective-permute-start.10 = (bf16[3,384,128]{2,1,0:T(8,128)(2,1)S(1)}, bf16[3,384,128]{2,1,0:T(8,128)(2,1)S(1)}, u32[]{:S(2)}, u32[]{:S(2)}) collective-permute-start(bf16[3,384,128]{2,1,0:T(8,128)(2,1)S(1)} %get-tuple-element.237), channel_id=1, source_target_pairs={{0,256},{8,264},{16,272},{24,280},{32,288},{40,296},{48,304},{56,3... | collective-permute-start | bytes 884744 | tf_op jit(solution)/shard_map/cond/branch_5_fun/ppermute | solution.py:291
  66.7 24.4 %collective-permute-done.10.theirs_ref = bf16[3,384,128]{2,1,0:T(8,128)(2,1)S(1)} collective-permute-done((bf16[3,384,128]{2,1,0:T(8,128)(2,1)S(1)}, bf16[3,384,128]{2,1,0:T(8,128)(2,1)S(1)}, u32[]{:S(2)}, u32[]{:S(2)}) %collective-permute-start.10) | collective-permute-done | bytes 294944 | tf_op jit(solution)/shard_map/cond/branch_5_fun/ppermute | solution.py:291
  91.2 0.8 average.1
Async XLA Ops:
  0.6 19.6 %copy-start.2 = (bf16[256,2048]{1,0:T(8,128)(2,1)S(1)}, bf16[256,2048]{1,0:T(8,128)(2,1)}, u32[]{:S(2)}) copy-start(bf16[256,2048]{1,0:T(8,128)(2,1)} %x_ref.1) | copy-start | bytes 3145732
  2.4 15.3 %all-to-all-start.6 = ((bf16[4,64,768]{2,1,0:T(8,128)(2,1)}), bf16[4,64,768]{2,1,0:T(8,128)(2,1)}, u32[]{:S(2)}, u32[]{:S(2)}) async-start(bf16[4,64,768]{2,1,0:T(8,128)(2,1)} %pack_weights.1), calls=%async_computation.6 | async-start | bytes 786432 | tf_op jit(solution)/shard_map/all_to_all | solution.py:335
  9.8 1.6 %copy-start = (bf16[256,4096]{1,0:T(8,128)(2,1)S(1)}, bf16[256,4096]{1,0:T(8,128)(2,1)}, u32[]{:S(2)}) copy-start(bf16[256,4096]{1,0:T(8,128)(2,1)} %r_ref.3) | copy-start | bytes 6291460
  11.3 0.7 copy-start.3
  12.1 0.7 copy-start.4
  12.8 7.5 %copy-start.1 = (bf16[256,4096]{1,0:T(8,128)(2,1)S(1)}, bf16[256,4096]{1,0:T(8,128)(2,1)}, u32[]{:S(2)}) copy-start(bf16[256,4096]{1,0:T(8,128)(2,1)} %r_ref.3) | copy-start | bytes 6291460
  20.3 3.7 %copy-start.5 = (f32[1,64,512]{2,1,0:T(8,128)S(1)}, f32[1,64,512]{2,1,0:T(8,128)}, u32[]{:S(2)}) copy-start(f32[1,64,512]{2,1,0:T(8,128)} %b_ref.1) | copy-start | bytes 393220
  52.5 38.6 %collective-permute-start.10 = (bf16[3,384,128]{2,1,0:T(8,128)(2,1)S(1)}, bf16[3,384,128]{2,1,0:T(8,128)(2,1)S(1)}, u32[]{:S(2)}, u32[]{:S(2)}) collective-permute-start(bf16[3,384,128]{2,1,0:T(8,128)(2,1)S(1)} %get-tuple-element.237), channel_id=1, source_target_pairs={{0,256},{8,264},{16,272},{24,280},{32,288},{40,296},{48,304},{56,3... | collective-permute-start | bytes 884744 | tf_op jit(solution)/shard_map/cond/branch_5_fun/ppermute | solution.py:291

commit v4 on v3

--- a/solution.py
+++ b/solution.py
@@ -93,7 +93,7 @@
     v = p + (nn(z16, m_high) + (nn(z16, m_middle) + nn(z16, m_low)))
     bw = jnp.sum(gram[RANK : RANK + 3, :RANK], axis=0, keepdims=True)
     rw = jnp.sum(p_ext[:, RANK : RANK + 3], axis=1, keepdims=True)
-    total = squares + jnp.sum(zf * (p + v), axis=1, keepdims=True)
+    total = jnp.maximum(squares + jnp.sum(zf * (p + v), axis=1, keepdims=True), 0.0)
     along = rw + jnp.sum(zf * bw, axis=1, keepdims=True)
     scale = lax.rsqrt(total * (1.0 / width) + 1e-05)
 
@@ -165,7 +165,7 @@
     weight = jnp.exp(score_col)
     tails = jnp.where(live[:1], jnp.sum(after * weight, axis=0, keepdims=True), 1.0)
     losses = jnp.where(live[:1], jnp.log(tails) - score_row[:1], 0.0)
-    loss_ref[0] = jnp.sum(losses)
+    loss_ref[...] = jnp.broadcast_to(jnp.sum(losses, axis=1, keepdims=True), loss_ref.shape)
     return jnp.sum(after * (weight / tails), axis=1, keepdims=True) - 1.0
 
 
@@ -204,7 +204,7 @@
     out_ref = refs[-1]
     for rows, first, cols in panels_of(refs[:6]):
         for i in range(3):
-            out_ref[i, rows, :] = refs[first + i][0, :, cols].astype(BF16)
+            out_ref[i, rows, :] = refs[first + i][0, :, cols].astype(out_ref.dtype)
 
 
 def update(ranks_ref, step_ref, terms_ref, *refs):
@@ -218,8 +218,9 @@
             packed_ref[i, rows, :] = value.astype(BF16)
 
 
-def average(theirs_ref, *refs):
-    mine, out = refs[:6], refs[6:]
+def average(theirs_ref, loss_tile_ref, *refs):
+    mine, out, loss_ref = refs[:6], refs[6:12], refs[12]
+    loss_ref[0] = loss_tile_ref[0, 0]
     for rows, first, cols in panels_of(mine):
         for i in range(3):
             out[first + i][0, :, cols] = 0.5 * (
@@ -236,8 +237,9 @@
         packed_ref[rows, :] = grad.astype(BF16)
 
 
-def own_update(step_ref, grad_ref, *refs):
-    state, out = refs[:6], refs[6:]
+def own_update(step_ref, grad_ref, loss_tile_ref, *refs):
+    state, out, loss_ref = refs[:6], refs[6:12], refs[12]
+    loss_ref[0] = loss_tile_ref[0, 0]
     for rows, first, cols in panels_of(state):
         old = [state[first + i][0, :, cols] for i in range(3)]
         for i, value in enumerate(adamw(step_ref[0] + 1, grad_ref[rows, :], *old)):
@@ -279,30 +281,37 @@
     rows = terms.shape[1] - TAIL
     kept = [shape(s.shape, F32) for s in state]
     loss_shape = shape((1,), F32)
+    loss_tile = shape((8, LANES), F32)
     terms = lax.all_to_all(terms, "fsdp", 0, 0)
     if replicas >> bit <= FAR:
         *mine, packed, loss = call(
             update,
-            kept + [shape((3, rows, LANES), BF16), loss_shape],
+            kept + [shape((3, rows, LANES), BF16), loss_tile],
             2,
             (ranks, step, terms) + state,
-            [VMEM] * 7 + [SMEM],
         )
         theirs = lax.ppermute(packed, "rep", swap)
-        mixed = call(average, kept, 0, (theirs,) + tuple(mine))
+        *mixed, loss = call(
+            average, kept + [loss_shape], 0, (theirs, loss) + tuple(mine), [VMEM] * 6 + [SMEM]
+        )
     else:
-        old = call(pack_state, shape((3, rows, LANES), BF16), 0, state)
+        kind = BF16 if replicas >> bit <= 2 * FAR else F32
+        old = call(pack_state, shape((3, rows, LANES), kind), 0, state)
         their_state = lax.ppermute(old, "rep", swap)
         grad, grad16, loss = call(
             gradient,
-            [shape((rows, LANES), F32), shape((rows, LANES), BF16), loss_shape],
+            [shape((rows, LANES), F32), shape((rows, LANES), BF16), loss_tile],
             1,
             (ranks, terms),
-            [VMEM, VMEM, SMEM],
         )
         their_grad = lax.ppermute(grad16, "rep", swap)
-        mine = call(
-            own_update, kept, 1, (step, grad) + state, cost=(rows * LANES * 40, rows * LANES * 24)
+        *mine, loss = call(
+            own_update,
+            kept + [loss_shape],
+            1,
+            (step, grad, loss) + state,
+            [VMEM] * 6 + [SMEM],
+            cost=(rows * LANES * 40, rows * LANES * 24),
         )
         mixed = call(their_update, kept, 1, (step, their_grad, their_state) + tuple(mine))
     new_a, new_ma, new_va, new_b, new_mb, new_vb = mixed

time: 92.5 us -> 63 us (0.68)
  the two profiles are of different devices: /device:TPU:40 before, /device:TPU:1 now
where the time goes in v4:
time: 63 us; the launch traced here: 62.5 us
  waiting for transfers between devices  20.5 us (33%)
  starting transfers between devices  18.2 us (29%)
  Pallas kernels  10.8 us (17%)
  blocking collectives  7.86 us (12%)
  local copies, waits for them, and re-layouts  3.04 us (5%)
  between operations  1.97 us (3%)
    all_to_all x1, waiting for transfers between devices, finish(): terms = lax.all_to_all(terms, 'fsdp', 0, 0)  15.8 us
    pallas_call x7, Pallas kernels, call(): pl.pallas_call(kernel, out_shape=out_shape, in_specs=[SMEM] * smem + [VME...  10.8 us
    all_gather x1, blocking collectives, per_device(): weights = lax.all_gather(across, 'fsdp', axis_index_groups=same_chip)  7.86 us
    all_to_all x1, starting transfers between devices, per_device(): across = lax.all_to_all(packed, 'fsdp', 0, 0, axis_index_groups=same_core)  6.44 us
    all_to_all x1, starting transfers between devices, finish(): terms = lax.all_to_all(terms, 'fsdp', 0, 0)  3.97 us
    ppermute x1, starting transfers between devices, finish(): their_state = lax.ppermute(old, 'rep', swap)  3.91 us
    ppermute x1, starting transfers between devices, finish(): their_grad = lax.ppermute(grad16, 'rep', swap)  3.88 us
    all_to_all x1, waiting for transfers between devices, per_device(): across = lax.all_to_all(packed, 'fsdp', 0, 0, axis_index_groups=same_core)  3.02 us
  transfers between devices with their start and end apart: 4, of which 3 were waited for; matrix products, arithmetic and copies ran while one was open for 0% of the time, Pallas kernels for 6%

profile of v4, /device:TPU:1, one launch (start us, length us, event | category | flops | bytes accessed | tf_op | source)
XLA Modules:
  0.0 62.5 jit_solution(18123789581524093086)
XLA Ops:
  0.6 0.0 copy-start.2
  0.6 1.8 %pack_weights.1 = bf16[4,64,768]{2,1,0:T(8,128)(2,1)} custom-call(f32[1,64,256]{2,1,0:T(8,128)} %a_ref.1, f32[1,64,512]{2,1,0:T(8,128)} %b_ref.1), custom_call_target="tpu_custom_call" | custom-call | tf_op jit(solution)/shard_map/pack_weights/pallas_call | solution.py:262
  2.4 6.4 %all-to-all-start.6 = ((bf16[4,64,768]{2,1,0:T(8,128)(2,1)}), bf16[4,64,768]{2,1,0:T(8,128)(2,1)}, u32[]{:S(2)}, u32[]{:S(2)}) async-start(bf16[4,64,768]{2,1,0:T(8,128)(2,1)} %pack_weights.1), calls=%async_computation.6 | async-start | bytes 786432 | tf_op jit(solution)/shard_map/all_to_all | solution.py:344
  10.2 0.0 copy-start
  10.2 1.6 %copy-done = bf16[256,4096]{1,0:T(8,128)(2,1)S(1)} copy-done((bf16[256,4096]{1,0:T(8,128)(2,1)S(1)}, bf16[256,4096]{1,0:T(8,128)(2,1)}, u32[]{:S(2)}) %copy-start) | copy-done | bytes 2097176
  11.8 0.0 copy-start.3
  11.8 0.7 %copy-done.3 = f32[4096]{0:T(1024)S(1)} copy-done((f32[4096]{0:T(1024)S(1)}, f32[4096]{0:T(1024)}, u32[]{:S(2)}) %copy-start.3) | copy-done | bytes 16408
  12.5 0.0 copy-start.4
  12.5 0.7 %copy-done.4 = bf16[4096]{0:T(1024)(128)(2,1)S(1)} copy-done((bf16[4096]{0:T(1024)(128)(2,1)S(1)}, bf16[4096]{0:T(1024)(128)(2,1)}, u32[]{:S(2)}) %copy-start.4) | copy-done | bytes 8216
  13.2 0.0 copy-start.1
  13.2 0.5 prepare.1
  13.7 3.0 %all-to-all-done.6 = bf16[4,64,768]{2,1,0:T(8,128)(2,1)} async-done(((bf16[4,64,768]{2,1,0:T(8,128)(2,1)}), bf16[4,64,768]{2,1,0:T(8,128)(2,1)}, u32[]{:S(2)}, u32[]{:S(2)}) %all-to-all-start.6) | async-done | bytes 393248 | tf_op jit(solution)/shard_map/all_to_all | solution.py:344
  16.7 7.9 %all-gather = bf16[8,64,768]{2,1,0:T(8,128)(2,1)S(1)} all-gather(bf16[4,64,768]{2,1,0:T(8,128)(2,1)} %all-to-all-done.6), channel_id=2, replica_groups={{0,1},{2,3},{4,5},{6,7},{8,9},{10,11},{12,13},{14,15},{16,17},{18,19},{..., dimensions={0}, use_global_device_ids=true | all-gather | bytes 1179648 | tf_op jit(solution)/shard_map/all_gather | solution.py:353
  24.6 0.0 copy-done.2
  24.6 0.0 copy-done.1
  24.6 0.0 copy-start.5
  24.6 3.7 %gradient_terms.1 = bf16[8,400,128]{2,1,0:T(8,128)(2,1)} custom-call(s32[1]{0:T(128)S(6)} %copy.62.length_ref, bf16[256,2048]{1,0:T(8,128)(2,1)S(1)} %copy-done.2, bf16[256,4096]{1,0:T(8,128)(2,1)S(1)} %copy-done.1, bf16[2,4,64,768]{3,2,1,0:T(8,128)(2,1)S(1)} %bitcast.4, f32[256,128]{1,0:T(8,128)S(1)} %get-tuple-element.267.squares_ref, ...), custom_call_target="tpu_custom_call" | custom-call | tf_op jit(solution)/shard_map/gradient_terms/pallas_call | solution.py:262
  28.3 0.0 copy-done.5
  28.3 34.1 %conditional.1 = (f32[1,64,256]{2,1,0:T(8,128)}, f32[1,64,512]{2,1,0:T(8,128)}, f32[1,64,256]{2,1,0:T(8,128)}, f32[1,64,256]{2,1,0:T(8,128)}, f32[1,64,512]{2,1,...) conditional(s32[]{:T(128)} %clamp.3, (bf16[8,400,128]{2,1,0:T(8,128)(2,1)}, ...), branch_computations={%region_0.1_spmd, %region_1.2_spmd, %region_2.3_spmd, %region_3.4_... | conditional | flops 1966080 | bytes 8225232 | solution.py:360
  28.3 0.0 copy-start.32
  28.3 0.0 copy-start.7
  28.3 0.0 copy-start.12
  28.3 0.0 copy-start.17
  28.4 0.0 copy-start.22
  28.4 0.0 copy-start.27
  28.4 4.0 %all-to-all-start.1 = ((bf16[8,400,128]{2,1,0:T(8,128)(2,1)}), bf16[8,400,128]{2,1,0:T(8,128)(2,1)S(1)}, u32[]{:S(2)}, u32[]{:S(2)}) async-start(bf16[8,400,128]{2,1,0:T(8,128)(2,1)} %get-tuple-element.135), calls=%async_computation.1 | async-start | bytes 1638400 | tf_op jit(solution)/shard_map/cond/branch_1_fun/all_to_all | solution.py:285
  32.3 1.1 %pack_state.6 = f32[3,384,128]{2,1,0:T(8,128)S(1)} custom-call(f32[1,64,256]{2,1,0:T(8,128)} %get-tuple-element.137.refs_0_, f32[1,64,256]{2,1,0:T(8,128)} %get-tuple-element.138.refs_1_, f32[1,64,256]{2,1,0:T(8,128)} %get-tuple-element.139.refs_2_, f32[1,64,512]{2,1,0:T(8,128)S(1)} %get-tuple-element.140.refs_3_, f32[1,64,512]{2,1,0:T(8,128)} %get-tuple-element.141.refs_4_, ...), custom_call_target="tpu_custom_call" | custom-call | tf_op jit(solution)/shard_map/cond/branch_1_fun/pack_state/pallas_call | solution.py:262
  33.5 3.9 %collective-permute-start.3 = (f32[3,384,128]{2,1,0:T(8,128)S(1)}, f32[3,384,128]{2,1,0:T(8,128)S(1)}, u32[]{:S(2)}, u32[]{:S(2)}) collective-permute-start(f32[3,384,128]{2,1,0:T(8,128)S(1)} %pack_state.6), channel_id=1, source_target_pairs={{0,16},{8,24},{16,0},{24,8},{32,48},{40,56},{48,32},{56,40},{64,80... | collective-permute-start | bytes 1769480 | tf_op jit(solution)/shard_map/cond/branch_1_fun/ppermute | solution.py:300
  37.4 15.8 %all-to-all-done.1.terms_ref = bf16[8,400,128]{2,1,0:T(8,128)(2,1)S(1)} async-done(((bf16[8,400,128]{2,1,0:T(8,128)(2,1)}), bf16[8,400,128]{2,1,0:T(8,128)(2,1)S(1)}, u32[]{:S(2)}, u32[]{:S(2)}) %all-to-all-start.1) | async-done | bytes 819232 | tf_op jit(solution)/shard_map/cond/branch_1_fun/all_to_all | solution.py:285
  53.2 0.0 copy-done.32
  53.2 0.8 %gradient.6 = (f32[384,128]{1,0:T(8,128)S(1)}, bf16[384,128]{1,0:T(8,128)(2,1)S(1)}, f32[8,128]{1,0:T(8,128)S(1)}) custom-call(s32[1,8]{1,0:T(1,128)S(1)} %copy-done.32, bf16[8,400,128]{2,1,0:T(8,128)(2,1)S(1)} %all-to-all-done.1.terms_ref), custom_call_target="tpu_custom_call" | custom-call | tf_op jit(solution)/shard_map/cond/branch_1_fun/gradient/pallas_call | solution.py:262
  54.0 3.9 %collective-permute-start.2 = (bf16[384,128]{1,0:T(8,128)(2,1)S(1)}, bf16[384,128]{1,0:T(8,128)(2,1)S(1)}, u32[]{:S(2)}, u32[]{:S(2)}) collective-permute-start(bf16[384,128]{1,0:T(8,128)(2,1)S(1)} %get-tuple-element.136), channel_id=1, source_target_pairs={{0,16},{8,24},{16,0},{24,8},{32,48},{40,56},{48,32},{56,40},{64,80... | collective-permute-start | bytes 294920 | tf_op jit(solution)/shard_map/cond/branch_1_fun/ppermute | solution.py:307
  57.9 0.0 copy-done.7
  57.9 0.0 copy-done.12
  57.9 0.0 copy-done.17
  57.9 0.0 copy-done.22
  57.9 0.0 copy-done.27
  57.9 1.2 %own_update.6 = (f32[1,64,256]{2,1,0:T(8,128)S(1)}, f32[1,64,256]{2,1,0:T(8,128)S(1)}, f32[1,64,256]{2,1,0:T(8,128)S(1)}, f32[1,64,512]{2,1,0:T(8,128)S(1)}, f32...) custom-call(s32[1]{0:T(128)} %get-tuple-element.133.step_ref, ...), custom_call_target="tpu_custom_call" | custom-call | flops 1966080 | bytes 1179648 | tf_op jit(solution)/shard_map/cond/branch_1_fun/own_update/pallas_call | solution.py:262
  59.2 0.0 collective-permute-done.3.state_ref
  59.2 1.7 %collective-permute-done.2.grad_ref = bf16[384,128]{1,0:T(8,128)(2,1)S(1)} collective-permute-done((bf16[384,128]{1,0:T(8,128)(2,1)S(1)}, bf16[384,128]{1,0:T(8,128)(2,1)S(1)}, u32[]{:S(2)}, u32[]{:S(2)}) %collective-permute-start.2) | collective-permute-done | bytes 98336 | tf_op jit(solution)/shard_map/cond/branch_1_fun/ppermute | solution.py:307
  60.9 1.6 %their_update.6 = (f32[1,64,256]{2,1,0:T(8,128)}, f32[1,64,256]{2,1,0:T(8,128)}, f32[1,64,256]{2,1,0:T(8,128)}, f32[1,64,512]{2,1,0:T(8,128)}, f32[1,64,512]{2,1,0:T(8,128)}, /*index=5*/f32[1,64,512]{2,1,0:T(8,128)}) custom-call(s32[1]{0:T(128)} %get-tuple-element.133.step_ref, bf16[384,128]{1,0:T(8,128)(2,1)S(1)} %collective-permute-done.2.grad_ref, ...), custom_call_target="tpu_custom_call" | custom-call | tf_op jit(solution)/shard_map/cond/branch_1_fun/their_update/pallas_call | solution.py:262
Async XLA Ops:
  0.6 24.0 %copy-start.2 = (bf16[256,2048]{1,0:T(8,128)(2,1)S(1)}, bf16[256,2048]{1,0:T(8,128)(2,1)}, u32[]{:S(2)}) copy-start(bf16[256,2048]{1,0:T(8,128)(2,1)} %x_ref.1) | copy-start | bytes 3145732
  2.4 14.3 %all-to-all-start.6 = ((bf16[4,64,768]{2,1,0:T(8,128)(2,1)}), bf16[4,64,768]{2,1,0:T(8,128)(2,1)}, u32[]{:S(2)}, u32[]{:S(2)}) async-start(bf16[4,64,768]{2,1,0:T(8,128)(2,1)} %pack_weights.1), calls=%async_computation.6 | async-start | bytes 786432 | tf_op jit(solution)/shard_map/all_to_all | solution.py:344
  10.2 1.6 %copy-start = (bf16[256,4096]{1,0:T(8,128)(2,1)S(1)}, bf16[256,4096]{1,0:T(8,128)(2,1)}, u32[]{:S(2)}) copy-start(bf16[256,4096]{1,0:T(8,128)(2,1)} %r_ref.3) | copy-start | bytes 6291460
  11.8 0.7 %copy-start.3 = (f32[4096]{0:T(1024)S(1)}, f32[4096]{0:T(1024)}, u32[]{:S(2)}) copy-start(f32[4096]{0:T(1024)} %param.30) | copy-start | bytes 49156
  12.5 0.7 %copy-start.4 = (bf16[4096]{0:T(1024)(128)(2,1)S(1)}, bf16[4096]{0:T(1024)(128)(2,1)}, u32[]{:S(2)}) copy-start(bf16[4096]{0:T(1024)(128)(2,1)} %param.29) | copy-start | bytes 24580
  13.2 11.4 %copy-start.1 = (bf16[256,4096]{1,0:T(8,128)(2,1)S(1)}, bf16[256,4096]{1,0:T(8,128)(2,1)}, u32[]{:S(2)}) copy-start(bf16[256,4096]{1,0:T(8,128)(2,1)} %r_ref.3) | copy-start | bytes 6291460
  24.6 3.7 %copy-start.5 = (f32[1,64,512]{2,1,0:T(8,128)S(1)}, f32[1,64,512]{2,1,0:T(8,128)}, u32[]{:S(2)}) copy-start(f32[1,64,512]{2,1,0:T(8,128)} %b_ref.1) | copy-start | bytes 393220
  28.3 24.9 %copy-start.32 = (s32[1,8]{1,0:T(1,128)S(1)}, s32[1,8]{1,0:T(1,128)}, u32[]{:S(2)}) copy-start(s32[1,8]{1,0:T(1,128)} %get-tuple-element.134.ranks_ref) | copy-start | bytes 100 | tf_op jit(solution)/shard_map/cond
  28.3 29.6 %copy-start.7 = (f32[1,64,512]{2,1,0:T(8,128)S(1)}, f32[1,64,512]{2,1,0:T(8,128)}, u32[]{:S(2)}) copy-start(f32[1,64,512]{2,1,0:T(8,128)} %get-tuple-element.141.refs_4_) | copy-start | bytes 393220 | tf_op jit(solution)/shard_map/cond
  28.3 29.6 %copy-start.12 = (f32[1,64,512]{2,1,0:T(8,128)S(1)}, f32[1,64,512]{2,1,0:T(8,128)}, u32[]{:S(2)}) copy-start(f32[1,64,512]{2,1,0:T(8,128)} %get-tuple-element.142.refs_5_) | copy-start | bytes 393220 | tf_op jit(solution)/shard_map/cond
  28.3 29.6 %copy-start.17 = (f32[1,64,256]{2,1,0:T(8,128)S(1)}, f32[1,64,256]{2,1,0:T(8,128)}, u32[]{:S(2)}) copy-start(f32[1,64,256]{2,1,0:T(8,128)} %get-tuple-element.137.refs_0_) | copy-start | bytes 196612 | tf_op jit(solution)/shard_map/cond
  28.4 29.6 %copy-start.22 = (f32[1,64,256]{2,1,0:T(8,128)S(1)}, f32[1,64,256]{2,1,0:T(8,128)}, u32[]{:S(2)}) copy-start(f32[1,64,256]{2,1,0:T(8,128)} %get-tuple-element.138.refs_1_) | copy-start | bytes 196612 | tf_op jit(solution)/shard_map/cond
  28.4 29.6 %copy-start.27 = (f32[1,64,256]{2,1,0:T(8,128)S(1)}, f32[1,64,256]{2,1,0:T(8,128)}, u32[]{:S(2)}) copy-start(f32[1,64,256]{2,1,0:T(8,128)} %get-tuple-element.139.refs_2_) | copy-start | bytes 196612 | tf_op jit(solution)/shard_map/cond
  28.4 24.8 %all-to-all-start.1 = ((bf16[8,400,128]{2,1,0:T(8,128)(2,1)}), bf16[8,400,128]{2,1,0:T(8,128)(2,1)S(1)}, u32[]{:S(2)}, u32[]{:S(2)}) async-start(bf16[8,400,128]{2,1,0:T(8,128)(2,1)} %get-tuple-element.135), calls=%async_computation.1 | async-start | bytes 1638400 | tf_op jit(solution)/shard_map/cond/branch_1_fun/all_to_all | solution.py:285
  33.5 25.7 %collective-permute-start.3 = (f32[3,384,128]{2,1,0:T(8,128)S(1)}, f32[3,384,128]{2,1,0:T(8,128)S(1)}, u32[]{:S(2)}, u32[]{:S(2)}) collective-permute-start(f32[3,384,128]{2,1,0:T(8,128)S(1)} %pack_state.6), channel_id=1, source_target_pairs={{0,16},{8,24},{16,0},{24,8},{32,48},{40,56},{48,32},{56,40},{64,80... | collective-permute-start | bytes 1769480 | tf_op jit(solution)/shard_map/cond/branch_1_fun/ppermute | solution.py:300
  54.0 6.9 %collective-permute-start.2 = (bf16[384,128]{1,0:T(8,128)(2,1)S(1)}, bf16[384,128]{1,0:T(8,128)(2,1)S(1)}, u32[]{:S(2)}, u32[]{:S(2)}) collective-permute-start(bf16[384,128]{1,0:T(8,128)(2,1)S(1)} %get-tuple-element.136), channel_id=1, source_target_pairs={{0,16},{8,24},{16,0},{24,8},{32,48},{40,56},{48,32},{56,40},{64,80... | collective-permute-start | bytes 294920 | tf_op jit(solution)/shard_map/cond/branch_1_fun/ppermute | solution.py:307
